TPU v7x, 512 devices: a whole 4x8x8 slice. The times are simulated.
512 devices in a mesh: atoms: 32 (over x_hi, z, core), kvec: 16 (over x_lo, y).
Axes of the slice: x: 4 (x_hi: 2, x_lo: 2; x = x_hi * 2 + x_lo), y: 8, z: 8, core: 2. Of those that a mesh axis runs over, the one named last changes fastest.
Arguments:
- positions: float32 [3, 65536], P(None, 'atoms'), may hold values from 0 to 1
- feats: float32 [64, 65536], P(None, 'atoms'), may hold values from -6 to 6
- species: int32 [65536], P('atoms'), may hold values from 0 to 15
- pad_count: int32 [256], P('atoms'), may hold values from 128 to 256
- k_lattice: int32 [3, 4096], P(None, 'kvec'), may hold values from -12 to 13, as said below
- filter_width: float32 [64], replicated, may hold values from 2e-05 to 0.002
- w_charge: float32 [64, 64], replicated, may hold values from -0.75 to 0.75
- species_embed: float32 [64, 16], replicated, may hold values from -3 to 3
- w_out: float32 [64, 64], replicated, may hold values from -0.75 to 0.75
- grad_out: float32 [64, 65536], P(None, ('atoms', 'kvec')), may hold values from -6 to 6
Outputs:
- message: float32 [64, 65536], P(None, ('atoms', 'kvec'))
- grad_positions: float32 [3, 65536], P(None, ('atoms', 'kvec'))
- grad_feats: float32 [64, 65536], P(None, ('atoms', 'kvec'))
Inputs may be any that keep to these rules, and one draw needn't show every extreme that they name: `k_lattice`: the 4096 columns are distinct nonzero integer vectors k with k[0] > 0, or k[0] = 0 and k[1] > 0, or k[0] = k[1] = 0 and k[2] > 0, and with squared length at most 169.
All inputs are finite; a program needn't handle non-finite values.
Results may differ from a plain program's by a relative error of at most 0.0003.
Values sent between devices are 32-bit elements; how exact they have to be, the bound alone decides.
A program may use at most 64 MiB of HBM per device.

v0:
```python
import math

import jax
import jax.numpy as jnp
from jax import lax
from jax.sharding import PartitionSpec as P

exact = lax.Precision.HIGHEST
two_pi = 2.0 * math.pi


def filtered_sum(part_cos, part_sin, filter_gain):
    sum_cos, sum_sin = lax.psum((part_cos, part_sin), "atoms")
    return (filter_gain * sum_cos, filter_gain * sum_sin)


def on_device(
    positions,
    feats,
    species,
    pad_count,
    k_lattice,
    filter_width,
    w_charge,
    species_embed,
    w_out,
    grad_out,
):
    kvec_count = lax.axis_size("kvec")
    atom_total = feats.shape[1] * lax.axis_size("atoms")
    atom_rows = feats.shape[1]
    share_rows = atom_rows // kvec_count
    valid_mask = (jnp.arange(atom_rows) % 256 < jnp.repeat(pad_count, 256)).astype(jnp.float32)
    one_hot = (jnp.arange(species_embed.shape[1])[:, None] == species[None, :]).astype(jnp.float32)
    charges = valid_mask[None, :] * (
        jnp.dot(w_charge.T, feats, precision=exact)
        + jnp.dot(species_embed, one_hot, precision=exact)
    )
    wave_vec = two_pi * k_lattice.astype(jnp.float32)
    k_square = jnp.sum(wave_vec * wave_vec, axis=0)
    filter_gain = (
        jnp.exp(-k_square[:, None] * filter_width[None, :])
        * 40.0
        / (k_square[:, None] + 40.0)
        / math.sqrt(atom_total)
    )
    phase = jnp.dot(positions.T, wave_vec, precision=exact)
    cos_tile = jnp.cos(phase)
    sine_tile = jnp.sin(phase)
    part_cos = jnp.einsum("aj,ca->jc", cos_tile, charges, precision=exact)
    part_sin = jnp.einsum("aj,ca->jc", sine_tile, charges, precision=exact)
    h_cos, h_sin = filtered_sum(part_cos, part_sin, filter_gain)
    first_row = lax.axis_index("kvec") * share_rows
    mask_share = lax.dynamic_slice_in_dim(valid_mask, first_row, share_rows, 0)
    field_full = jnp.einsum("aj,jc->ca", cos_tile, h_cos, precision=exact) + jnp.einsum(
        "aj,jc->ca", sine_tile, h_sin, precision=exact
    )
    field_part = lax.psum_scatter(field_full, "kvec", scatter_dimension=1, tiled=True)
    field_out = mask_share[None, :] * field_part
    message = jnp.dot(w_out.T, field_out, precision=exact)
    cotangent = lax.all_gather(grad_out, "kvec", axis=1, tiled=True)
    adjoint = valid_mask[None, :] * jnp.dot(w_out, cotangent, precision=exact)
    e_cos = jnp.einsum("aj,ca->jc", cos_tile, adjoint, precision=exact)
    e_sin = jnp.einsum("aj,ca->jc", sine_tile, adjoint, precision=exact)
    b_cos, b_sin = filtered_sum(e_cos, e_sin, filter_gain)
    charge_grad = jnp.einsum("aj,jc->ca", cos_tile, b_cos, precision=exact) + jnp.einsum(
        "aj,jc->ca", sine_tile, b_sin, precision=exact
    )
    along_sin = jnp.einsum("ca,jc->aj", adjoint, h_sin, precision=exact) + jnp.einsum(
        "ca,jc->aj", charges, b_sin, precision=exact
    )
    along_cos = jnp.einsum("ca,jc->aj", adjoint, h_cos, precision=exact) + jnp.einsum(
        "ca,jc->aj", charges, b_cos, precision=exact
    )
    dphase = cos_tile * along_sin - sine_tile * along_cos
    force_part = jnp.einsum("xj,aj->xa", wave_vec, dphase, precision=exact)
    grad_share, force_share = (
        lax.psum_scatter(charge_grad, "kvec", scatter_dimension=1, tiled=True),
        lax.psum_scatter(force_part, "kvec", scatter_dimension=1, tiled=True),
    )
    grad_feats = jnp.dot(w_charge, mask_share[None, :] * grad_share, precision=exact)
    return (message, force_share, grad_feats)


def solution(mesh):
    placed = (
        P(None, "atoms"),
        P(None, "atoms"),
        P("atoms"),
        P("atoms"),
        P(None, "kvec"),
        P(),
        P(),
        P(),
        P(),
        P(None, ("atoms", "kvec")),
    )
    return jax.shard_map(
        on_device,
        mesh=mesh,
        in_specs=placed,
        out_specs=(
            P(None, ("atoms", "kvec")),
            P(None, ("atoms", "kvec")),
            P(None, ("atoms", "kvec")),
        ),
        check_vma=False,
    )
```

profile of v0, /device:TPU:1, one launch (start us, length us, event | category | flops | bytes accessed | tf_op | source)
XLA Modules:
  0.0 567.7 jit_solution(11806230533957962040)
XLA Ops:
  7.2 0.0 copy-start
  7.2 0.0 all-reduce.3.cloned.1.call-start
  7.2 0.8 broadcast_bitcast_fusion
  8.0 30.6 %all_gather.3 = f32[64,2048]{1,0:T(8,128)S(1)} all-gather(f32[64,128]{1,0:T(8,128)} %param.19), channel_id=1, replica_groups=mesh['atoms'=32,'kvec'=16] {'kvec'}, dimensions={1}, use_global_device_ids=true | all-gather | bytes 557056 | tf_op jit(solution)/shard_map/all_gather | solution.py:61
  38.6 1.1 convolution_bitcast_fusion.1
  39.7 0.0 copy-start.10
  39.7 9.7 %fusion.51 = (f32[256,2048]{1,0:T(8,128)S(1)}, f32[256,2048]{1,0:T(8,128)S(1)}) fusion(f32[3,2048]{1,0:T(4,128)} %param.10, s32[3,256]{1,0:T(4,128)} %param.14), kind=kOutput, calls=%fused_computation.61 | convolution fusion | flops 18875904 | bytes 4221952 | tf_op jit(solution)/shard_map/dot_general | solution.py:47
  49.5 0.0 copy-done.10
  49.5 0.0 copy-start.1
  49.5 0.0 copy-start.11
  49.5 0.6 convolution_multiply_fusion
  50.1 0.0 copy-start.3
  50.1 2.6 fusion.55
  52.7 0.0 copy-done.11
  52.7 0.6 fusion.3
  53.4 2.8 fusion.54
  56.2 0.0 copy-done.3
  56.2 2.6 fusion.56
  58.9 2.7 fusion.53
  61.5 0.0 all-reduce.3.cloned.1.call-update
  61.5 0.0 reduce-scatter.10.cloned.1.call-start
  61.6 0.0 copy-done.12
  61.6 277.5 %all-reduce.3.cloned.1.call-done = (f32[256,64]{0,1:T(8,128)}, f32[256,64]{0,1:T(8,128)}, f32[256,64]{0,1:T(8,128)}, f32[256,64]{0,1:T(8,128)}) async-done(((f32[256,64]{0,1:T(8,128)}, f32[256,64]{0,1:T(8,128)}, f32[256,64]{0,1:T(8,128)}, f32[256,64]{0,1:T(8,128)}), (f32[256,64]{0,1:T(8,128)}, f32[256,64]{0,1:T(8,128)}, f32[256,64]{0,1:T(8,128)}, f32[256,64]{0,1:T(8,128)})) %all-reduce.3.cloned.1.call-update) | async-done | bytes 262160 | tf_op jit(solution)/shard_map/psum | solution.py:13
  339.1 0.0 copy-done.13
  339.1 3.9 fusion.13
  343.1 0.0 copy-done.9
  343.1 1.9 fusion.11
  345.0 1.9 fusion.15
  347.0 2.2 fusion.2
  349.1 2.2 fusion.1
  351.4 0.0 copy-start.5
  351.4 4.4 convolution_bitcast_fusion
  355.8 0.0 reduce-scatter.10.cloned.1.call-update
  355.8 0.3 reduce-scatter.6.cloned.1.call-start
  356.1 0.0 copy-done.5
  356.1 2.2 convolution_add_fusion.3
  358.3 0.0 reduce-scatter.6.cloned.1.call-update
  358.3 0.0 reduce-scatter.8.cloned.1.call-start
  358.4 3.0 fusion.20
  361.4 2.2 convolution_add_fusion.2
  363.6 0.0 reduce-scatter.8.cloned.1.call-update
  363.6 0.1 dynamic_slice.3
  363.7 52.7 %reduce-scatter.10.cloned.1.call-done = f32[128,3]{1,0:T(8,128)} async-done(((f32[2048,3]{1,0:T(8,128)}), f32[128,3]{1,0:T(8,128)}) %reduce-scatter.10.cloned.1.call-update) | async-done | bytes 1552
  416.4 1.5 copy.14
  417.9 69.8 %reduce-scatter.6.cloned.1.call-done = f32[64,128]{1,0:T(8,128)} async-done(((f32[64,2048]{1,0:T(8,128)}), f32[64,128]{1,0:T(8,128)}) %reduce-scatter.6.cloned.1.call-update) | async-done | bytes 32784 | tf_op jit(solution)/shard_map/reduce_scatter | solution.py:58
  487.7 1.6 convolution_bitcast_fusion.3
  489.3 70.3 %reduce-scatter.8.cloned.1.call-done = f32[64,128]{1,0:T(8,128)} async-done(((f32[64,2048]{1,0:T(8,128)}), f32[64,128]{1,0:T(8,128)}) %reduce-scatter.8.cloned.1.call-update) | async-done | bytes 32784 | tf_op jit(solution)/shard_map/reduce_scatter | solution.py:78
  559.7 1.5 convolution_bitcast_fusion.2
  (19 shorter events, 0.1 us)
Async XLA Ops:
  7.2 45.6 %copy-start = (f32[64,2048]{1,0:T(8,128)S(1)}, f32[64,2048]{1,0:T(8,128)}, u32[]{:S(2)}) copy-start(f32[64,2048]{1,0:T(8,128)} %param.11) | copy-start | bytes 1572868
  7.2 332.0 %all-reduce.3.cloned.1.call-start = ((), (), s32[]{:S(2)}) async-start(), calls=%async_computation.6 | async-start | bytes 524288 | tf_op jit(solution)/shard_map/psum | solution.py:13
  39.7 9.7 %copy-start.10 = (f32[64,64]{1,0:T(8,128)S(1)}, f32[64,64]{1,0:T(8,128)}, u32[]{:S(2)}) copy-start(f32[64,64]{1,0:T(8,128)} %param.18) | copy-start | bytes 49156
  49.5 9.4 %copy-start.1 = (f32[256,2048]{1,0:T(8,128)}, f32[256,2048]{1,0:T(8,128)S(1)}, u32[]{:S(2)}) copy-start(f32[256,2048]{1,0:T(8,128)S(1)} %get-tuple-element.8) | copy-start | bytes 6291460
  49.5 3.3 copy-start.11
  50.1 6.1 %copy-start.3 = (f32[64,2048]{1,0:T(8,128)}, f32[64,2048]{1,0:T(8,128)S(1)}, u32[]{:S(2)}) copy-start(f32[64,2048]{1,0:T(8,128)S(1)} %convolution_multiply_fusion) | copy-start | bytes 1572868
  58.9 2.7 copy-start.12
  58.9 280.3 %copy-start.13 = (f32[64]{0:T(128)S(1)}, f32[64]{0:T(128)}, u32[]{:S(2)}) copy-start(f32[64]{0:T(128)} %param.15) | copy-start | bytes 772
  61.5 354.9 %reduce-scatter.10.cloned.1.call-start = ((), (), s32[]{:S(2)}) async-start(), calls=%async_computation.5 | async-start | bytes 1114112
  339.1 3.9 copy-start.4
  339.1 3.9 copy-start.9
  339.1 5.9 %copy-start.8 = (f32[256,64]{0,1:T(8,128)S(1)}, f32[256,64]{0,1:T(8,128)}, u32[]{:S(2)}) copy-start(f32[256,64]{0,1:T(8,128)} %get-tuple-element.4) | copy-start | bytes 196612
  343.1 3.9 copy-start.2
  343.1 3.9 copy-start.6
  346.9 2.2 copy-start.7
  351.4 4.7 copy-start.5
  355.8 131.9 %reduce-scatter.6.cloned.1.call-start = ((), (), s32[]{:S(2)}) async-start(), calls=%async_computation.3 | async-start | bytes 557056 | tf_op jit(solution)/shard_map/reduce_scatter | solution.py:58
  358.3 201.3 %reduce-scatter.8.cloned.1.call-start = ((), (), s32[]{:S(2)}) async-start(), calls=%async_computation.4 | async-start | bytes 557056 | tf_op jit(solution)/shard_map/reduce_scatter | solution.py:78
Sparse Core Ops, SparseCore 0:
  61.7 277.4 all-reduce.2
  355.9 60.4 reduce-scatter.9
  419.2 68.4 reduce-scatter.5
  490.6 69.0 reduce-scatter.7
where the time goes:
time: 579 us; the launch traced here: 568 us
  waiting for transfers between devices  470 us (81%)
  matrix products  49.9 us (9%)
  blocking collectives  30.6 us (5%)
  between operations  14 us (2%)
    psum x1, waiting for transfers between devices, filtered_sum(): sum_cos, sum_sin = lax.psum((part_cos, part_sin), 'atoms')  278 us
    reduce_scatter x1, waiting for transfers between devices, on_device(): lax.psum_scatter(charge_grad, 'kvec', scatter_dimension=1, tiled=True)  70.3 us
    reduce_scatter x1, waiting for transfers between devices, on_device(): lax.psum_scatter(field_full, 'kvec', scatter_dimension=1, tiled=True)  69.8 us
    unnamed x5, waiting for transfers between devices  52.8 us
    all_gather x1, blocking collectives, on_device(): cotangent = lax.all_gather(grad_out, 'kvec', axis=1, tiled=True)  30.6 us
  transfers between devices with their start and end apart: 4, of which 4 were waited for; matrix products, arithmetic and copies ran while one was open for 2% of the time, Pallas kernels for 0%

commit v1 on v0

v1 whole, which is shorter than its diff:
```python
import functools
import math

import jax
import jax.numpy as jnp
import numpy as np
from jax import lax
from jax.experimental import pallas as pl
from jax.experimental.pallas import tpu as pltpu
from jax.sharding import PartitionSpec as P

MESH = pl.DeviceIdType.MESH
exact = lax.Precision.HIGHEST
two_pi = 2.0 * math.pi
f32 = jnp.float32
bf16 = jnp.bfloat16

A = 1024
K = 512
H = 256
CH = 64
S = 128


def fit_poly(fn, count, points=2000):
    nodes = 0.25 * (np.cos(np.pi * (np.arange(points) + 0.5) / points) + 1.0) * 0.5
    table = np.vander(nodes / 0.25, count, increasing=True)
    coef = np.linalg.lstsq(table, fn(np.sqrt(nodes)), rcond=None)[0]
    return [float(c) / 0.25**n for n, c in enumerate(coef)]


sin_coef = fit_poly(lambda u: 2.0 * np.sin(np.pi * u) / u, 5)
cos_coef = fit_poly(lambda u: np.cos(np.pi * u), 5)


def horner(coef, sq):
    total = coef[-1]
    for c in coef[-2::-1]:
        total = total * sq + c
    return total


def sin_cos_turns(t):
    u = t - jnp.round(t)
    sq = u * u
    twice_sin = u * horner(sin_coef, sq)
    cos_half = horner(cos_coef, sq)
    return 1.0 - 0.5 * (twice_sin * twice_sin), twice_sin * cos_half


def split(value):
    high = value.astype(bf16)
    return high, (value - high.astype(f32)).astype(bf16)


def dot(a, b, dims=((1,), (0,)), precision=None):
    return lax.dot_general(a, b, (dims, ((), ())), precision=precision, preferred_element_type=f32)


def middle_out(i, n):
    return n // 2 + ((i + 1) // 2) * (1 - 2 * (i % 2))


def kernel(
    pos_ref, feats_ref, species_ref, pad_ref, k_ref, width_ref, wq_ref, embed_ref, wo_ref, grad_ref,
    message_ref, force_ref, gfeat_ref,
    feats, kall, kcol, kmat, xmat, mask, t_hi, t_lo, cos_f, sin_f, charge, cots, adjoint,
    part, core_in, core_sum, ring_in, owned, table, out_y, in_y, out_f, in_f,
    feats_sem, k_sem, cot_send, cot_recv, core_sem, plane_send, plane_recv, table_send, table_recv,
    y_send, y_recv, f_send, f_recv,
):
    atoms_at = lax.axis_index("atoms")
    kvec_at = lax.axis_index("kvec")
    core, z, x_hi = atoms_at % 2, (atoms_at // 2) % 8, atoms_at // 16
    x_lo, y = kvec_at // 8, kvec_at % 8
    x = x_hi * 2 + x_lo
    me = x * 8 + z

    def on_y(other):
        return (atoms_at, x_lo * 8 + other)

    def on_plane(px, pz):
        return ((px // 2) * 16 + pz * 2 + core, (px % 2) * 8 + y)

    sibling = (atoms_at + 1 - 2 * core, kvec_at)
    partner = (atoms_at, (1 - x_lo) * 8 + y)

    def plane_loop(body):
        def step(i, _):
            px = (x + middle_out(i // 8, 4)) % 4
            pz = (z + middle_out(i % 8, 8)) % 8
            body(px, pz, px * 8 + pz)
            return 0

        lax.fori_loop(0, 31, step, 0)

    def y_loop(body):
        def step(i, _):
            body((y + middle_out(i, 8)) % 8)
            return 0

        lax.fori_loop(0, 7, step, 0)

    def remote(src, dst, send, recv, device):
        return pltpu.make_async_remote_copy(
            src_ref=src, dst_ref=dst, send_sem=send, recv_sem=recv, device_id=device, device_id_type=MESH
        )

    barrier = pltpu.get_barrier_semaphore()

    def greet(device):
        pl.semaphore_signal(barrier, inc=1, device_id=device, device_id_type=MESH)

    plane_loop(lambda px, pz, p: greet(on_plane(px, pz)))
    y_loop(lambda other: greet(on_y(other)))
    greet(sibling)

    feats_copy = pltpu.make_async_copy(
        feats_ref.at[:, pl.ds(pl.multiple_of(x_lo * A, A), A)], feats, feats_sem
    )
    feats_copy.start()

    kall[x_lo] = jnp.concatenate([k_ref[...].astype(f32), jnp.zeros((5, H), f32)], axis=0)
    pos = pos_ref[:, pl.ds(pl.multiple_of(x_lo * A, A), A)]
    pos = jnp.concatenate([pos, jnp.zeros((5, A), f32)], axis=0)
    pos_hi = pos.astype(bf16).astype(f32)
    pos_mid = (pos - pos_hi).astype(bf16).astype(f32)
    pos_low = (pos - pos_hi) - pos_mid
    xmat[...] = jnp.concatenate([pos_hi, pos_mid, pos_low, jnp.zeros((8, A), f32)], axis=0).astype(bf16)
    lanes = lax.broadcasted_iota(jnp.int32, (1, 256), 1)
    for block in range(4):
        mask[:, block * 256 : (block + 1) * 256] = (lanes < pad_ref[x_lo * 4 + block]).astype(f32)

    def trig_half(q):
        kt = kall[q].T
        kcol[pl.ds(pl.multiple_of(q * H, H), H), :] = kt
        kmat[pl.ds(pl.multiple_of(q * H, H), H), :] = jnp.concatenate([kt] * 4, axis=1).astype(bf16)

        def step(i, _):
            rows = pl.ds(pl.multiple_of(q * H + i * 32, 32), 32)
            rows_sin = pl.ds(pl.multiple_of(K + q * H + i * 32, 32), 32)
            left = kmat[rows, :]
            for part_at in range(4):
                cols = slice(part_at * 256, (part_at + 1) * 256)
                cos, sin = sin_cos_turns(dot(left, xmat[:, cols]))
                cos_f[rows, cols] = cos
                sin_f[rows, cols] = sin
                high, low = split(cos)
                t_hi[rows, cols] = high
                t_lo[rows, cols] = low
                high, low = split(sin)
                t_hi[rows_sin, cols] = high
                t_lo[rows_sin, cols] = low
            return 0

        lax.fori_loop(0, H // 32, step, 0)

    low_lanes = lax.broadcasted_iota(jnp.int32, (1, 128), 1) < CH

    def factors(which, q, quant):
        both = quant[...]
        for i in range(2):
            base = q * H + i * 128
            found = []
            for offset in (0, K):
                rows = pl.ds(pl.multiple_of(offset + base, 128), 128)
                one = dot(t_hi[rows, :], both, ((1,), (1,))) + dot(t_lo[rows, :], both, ((1,), (1,)))
                found.append(one + pltpu.roll(one, CH, 1))
            part[which, pl.ds(pl.multiple_of(base, 128), 128), :] = jnp.where(low_lanes, found[0], found[1])

    trig_half(x_lo)

    feats_copy.wait()
    one_hot = (
        lax.broadcasted_iota(jnp.int32, (16, A), 0) == species_ref[:, pl.ds(pl.multiple_of(x_lo * A, A), A)]
    ).astype(f32)
    q_high, q_low = split(
        mask[...]
        * (
            dot(wq_ref[...], feats[...], ((0,), (0,)), exact)
            + dot(embed_ref[...], one_hot, precision=exact)
        )
    )
    charge[0:CH, :] = q_high
    charge[CH:128, :] = q_low
    factors(0, x_lo, charge)

    pl.semaphore_wait(barrier, 39)

    k_copy = remote(kall.at[x_lo], kall.at[x_lo], k_sem.at[0], k_sem.at[1], partner)
    k_copy.start()

    def cot_copy(other, slot):
        return remote(grad_ref, cots.at[slot], cot_send.at[other], cot_recv.at[slot], on_y(other))

    y_loop(lambda other: cot_copy(other, y).start())
    cots[y] = grad_ref[...]

    remote(kall.at[1 - x_lo], kall.at[1 - x_lo], k_sem.at[0], k_sem.at[1], partner).wait_recv()
    trig_half(1 - x_lo)
    factors(0, 1 - x_lo, charge)

    def core_copy(which, stage, src, dst):
        return remote(src, dst, core_sem.at[0, which, stage], core_sem.at[1, which, stage], sibling)

    own_rows = pl.ds(pl.multiple_of(core * H, H), H)
    other_rows = pl.ds(pl.multiple_of((1 - core) * H, H), H)

    def pair_sum_copy(which):
        return core_copy(which, 0, part.at[which, other_rows, :], core_in.at[which])

    def share_rows(p):
        return pl.ds(pl.multiple_of(p * 8, 8), 8)

    def plane_copy(which, px, pz, p, slot):
        return remote(
            core_sum.at[which, share_rows(p), :], ring_in.at[which, slot],
            plane_send.at[which, p], plane_recv.at[which, slot], on_plane(px, pz),
        )

    def scatter_start(which):
        pair_sum_copy(which).wait_recv()
        core_sum[which] = part[which, own_rows, :] + core_in[which]
        plane_loop(lambda px, pz, p: plane_copy(which, px, pz, p, me).start())
        ring_in[which, me] = core_sum[which, share_rows(me), :]

    def table_rows(p):
        return pl.ds(pl.multiple_of(core * H + p * 8, 8), 8)

    def table_copy(which, px, pz, p, slot):
        return remote(
            owned.at[which], table.at[which, table_rows(slot), :],
            table_send.at[which, p], table_recv.at[which, slot], on_plane(px, pz),
        )

    def gather_start(which):
        plane_loop(lambda px, pz, p: plane_copy(which, px, pz, p, p).wait_recv())
        total = ring_in[which, 0]
        for p in range(1, 32):
            total = total + ring_in[which, p]
        wave = two_pi * kcol[table_rows(me), :]
        square = jnp.sum(wave * wave, axis=1, keepdims=True)
        width = width_ref[...]
        width = jnp.concatenate([width, width], axis=1)
        gain = jnp.exp(-square * width) * 40.0 / (square + 40.0) / 256.0
        owned[which] = gain * total
        plane_loop(lambda px, pz, p: table_copy(which, px, pz, p, me).start())
        table[which, table_rows(me), :] = owned[which]

    def pair_share_copy(which, rows):
        return core_copy(which, 1, table.at[which, rows, :], table.at[which, rows, :])

    def gather_end(which):
        plane_loop(lambda px, pz, p: table_copy(which, px, pz, p, p).wait_recv())
        pair_share_copy(which, own_rows).start()
        pair_share_copy(which, other_rows).wait_recv()

    pair_sum_copy(0).start()
    scatter_start(0)

    y_loop(lambda other: cot_copy(other, other).wait_recv())
    for s in range(8):
        cols = slice(s * S, (s + 1) * S)
        high, low = split(mask[:, cols] * dot(wo_ref[...], cots[s], precision=exact))
        adjoint[0:CH, cols] = high
        adjoint[CH:128, cols] = low
    factors(1, 0, adjoint)
    factors(1, 1, adjoint)
    pair_sum_copy(1).start()
    scatter_start(1)

    gather_start(0)
    gather_start(1)

    def y_copy(which, other, slot):
        return remote(
            out_y.at[which, other], in_y.at[which, slot], y_send.at[which, other], y_recv.at[which, slot], on_y(other)
        )

    def fields(which):
        high, low = split(table[which].T)
        left = jnp.concatenate(
            [
                jnp.concatenate([high[0:CH], high[CH:128]], axis=1),
                jnp.concatenate([low[0:CH], low[CH:128]], axis=1),
            ],
            axis=0,
        )
        for at in range(4):
            cols = slice(at * 256, (at + 1) * 256)
            both = dot(left, t_hi[:, cols]) + dot(left, t_lo[:, cols])
            field = both[0:CH] + both[CH:128]
            out_y[which, 2 * at] = field[:, 0:S]
            out_y[which, 2 * at + 1] = field[:, S:256]
        y_loop(lambda other: y_copy(which, other, y).start())
        in_y[which, y] = out_y[which, y]

    def forces(which, quant, add):
        high, low = split(table[which])
        high, low = high.astype(f32), low.astype(f32)
        sin_side = jnp.where(low_lanes, pltpu.roll(high, CH, 1), low).astype(bf16)
        cos_side = jnp.where(low_lanes, high, pltpu.roll(low, CH, 1)).astype(bf16)
        sin_side = jnp.concatenate([sin_side, sin_side], axis=1)
        cos_side = jnp.concatenate([cos_side, cos_side], axis=1)
        columns = [kcol[:, n : n + 1] for n in range(3)]
        for at in range(4):
            cols = slice(at * 256, (at + 1) * 256)
            high_q, low_q = quant[0:CH, cols], quant[CH:128, cols]
            right = jnp.concatenate([high_q, high_q, low_q, low_q], axis=0)
            turn = cos_f[:, cols] * dot(sin_side, right) - sin_f[:, cols] * dot(cos_side, right)
            rows = [jnp.sum(column * turn, axis=0, keepdims=True) for column in columns]
            rows = jnp.concatenate(rows + [jnp.zeros((5, 256), f32)], axis=0)
            for half in range(2):
                slot = 2 * at + half
                here = rows[:, half * S : (half + 1) * S]
                out_f[slot] = out_f[slot] + here if add else here

    def f_copy(other, slot):
        return remote(out_f.at[other], in_f.at[slot], f_send.at[other], f_recv.at[slot], on_y(other))

    gather_end(0)
    fields(0)
    forces(0, adjoint, False)
    gather_end(1)
    fields(1)
    forces(1, charge, True)
    y_loop(lambda other: f_copy(other, y).start())
    in_f[y] = out_f[y]

    share = mask[:, pl.ds(pl.multiple_of(y * S, S), S)]

    def collect(which):
        y_loop(lambda other: y_copy(which, other, other).wait_recv())
        total = in_y[which, 0]
        for s in range(1, 8):
            total = total + in_y[which, s]
        return share * total

    message_ref[...] = dot(wo_ref[...], collect(0), ((0,), (0,)), exact)
    gfeat_ref[...] = dot(wq_ref[...], collect(1), precision=exact)
    y_loop(lambda other: f_copy(other, other).wait_recv())
    total = in_f[0]
    for s in range(1, 8):
        total = total + in_f[s]
    force_ref[...] = (two_pi * total)[0:3, :]

    k_copy.wait_send()
    y_loop(lambda other: cot_copy(other, y).wait_send())
    for which in range(2):
        pair_sum_copy(which).wait_send()
        pair_share_copy(which, own_rows).wait_send()
        plane_loop(lambda px, pz, p: plane_copy(which, px, pz, p, me).wait_send())
        plane_loop(lambda px, pz, p: table_copy(which, px, pz, p, me).wait_send())
        y_loop(lambda other: y_copy(which, other, y).wait_send())
    y_loop(lambda other: f_copy(other, y).wait_send())


def on_device(
    positions, feats, species, pad_count, k_lattice, filter_width, w_charge, species_embed, w_out, grad_out
):
    vmem = pl.BlockSpec(memory_space=pltpu.VMEM)
    dma = pltpu.SemaphoreType.DMA
    return pl.pallas_call(
        kernel,
        out_shape=(
            jax.ShapeDtypeStruct((CH, S), f32),
            jax.ShapeDtypeStruct((3, S), f32),
            jax.ShapeDtypeStruct((CH, S), f32),
        ),
        in_specs=[
            vmem,
            pl.BlockSpec(memory_space=pl.ANY),
            vmem,
            pl.BlockSpec(memory_space=pltpu.SMEM),
            vmem, vmem, vmem, vmem, vmem, vmem,
        ],
        out_specs=(vmem, vmem, vmem),
        scratch_shapes=[
            pltpu.VMEM((CH, A), f32),
            pltpu.VMEM((2, 8, H), f32),
            pltpu.VMEM((K, 8), f32),
            pltpu.VMEM((K, 32), bf16),
            pltpu.VMEM((32, A), bf16),
            pltpu.VMEM((1, A), f32),
            pltpu.VMEM((2 * K, A), bf16),
            pltpu.VMEM((2 * K, A), bf16),
            pltpu.VMEM((K, A), f32),
            pltpu.VMEM((K, A), f32),
            pltpu.VMEM((128, A), bf16),
            pltpu.VMEM((8, CH, S), f32),
            pltpu.VMEM((128, A), bf16),
            pltpu.VMEM((2, K, 128), f32),
            pltpu.VMEM((2, H, 128), f32),
            pltpu.VMEM((2, H, 128), f32),
            pltpu.VMEM((2, 32, 8, 128), f32),
            pltpu.VMEM((2, 8, 128), f32),
            pltpu.VMEM((2, K, 128), f32),
            pltpu.VMEM((2, 8, CH, S), f32),
            pltpu.VMEM((2, 8, CH, S), f32),
            pltpu.VMEM((8, 8, S), f32),
            pltpu.VMEM((8, 8, S), f32),
            dma, dma((2,)), dma((8,)), dma((8,)), dma((2, 2, 2)),
            dma((2, 32)), dma((2, 32)), dma((2, 32)), dma((2, 32)),
            dma((2, 8)), dma((2, 8)), dma((8,)), dma((8,)),
        ],
        name="ewald",
        compiler_params=pltpu.CompilerParams(
            collective_id=0, has_side_effects=True, vmem_limit_bytes=40 * 1024 * 1024
        ),
    )(
        positions, feats, species.reshape(1, -1), pad_count, k_lattice, filter_width.reshape(1, -1),
        w_charge, species_embed, w_out, grad_out,
    )


def solution(mesh):
    placed = (
        P(None, "atoms"),
        P(None, "atoms"),
        P("atoms"),
        P("atoms"),
        P(None, "kvec"),
        P(),
        P(),
        P(),
        P(),
        P(None, ("atoms", "kvec")),
    )
    return jax.shard_map(
        on_device,
        mesh=mesh,
        in_specs=placed,
        out_specs=(P(None, ("atoms", "kvec")),) * 3,
        check_vma=False,
    )
```

time: 579 us -> 71.6 us (0.12); the launches traced: 568 us -> 71.1 us
  waiting for transfers between devices: 470 us -> 0 us
  Pallas kernels: 0 us -> 63.8 us
  matrix products: 49.9 us -> 0 us
  blocking collectives: 30.6 us -> 0 us
  between operations: 14 us -> 0.71 us
    psum x1 -> x0, waiting for transfers between devices: 278 us -> none  [filtered_sum(): sum_cos, sum_sin = lax.psum((part_cos, part_sin), 'atoms')]
    reduce_scatter x2 -> x0, waiting for transfers between devices: 140 us -> none  [the longest x1 70.3 us: on_device(): lax.psum_scatter(charge_grad, 'kvec', scatter_dimension=1, tiled=True)]
    pallas_call x0 -> x1, Pallas kernels: none -> 63.8 us  [on_device(): pl.pallas_call(kernel, out_shape=(jax.ShapeDtypeStruct((CH, S), f32), jax...]
    unnamed x5 -> x0, waiting for transfers between devices: 52.8 us -> none
    dot_general x18 -> x0, matrix products: 45.5 us -> none  [the longest x1 9.7 us: on_device(): phase = jnp.dot(positions.T, wave_vec, precision=exact)]
    all_gather x1 -> x0, blocking collectives: 30.6 us -> none  [on_device(): cotangent = lax.all_gather(grad_out, 'kvec', axis=1, tiled=True)]
  transfers between devices with their start and end apart: 4 -> 0, of which waited for: 4 -> 0; matrix products, arithmetic and copies ran while one was open for 2% -> 0% of each run, Pallas kernels for 0% -> 0%
where the time goes in v1:
time: 71.6 us; the launch traced here: 71.1 us
  Pallas kernels  63.8 us (89%)
  local copies, waits for them, and re-layouts  6.62 us (9%)
    pallas_call x1, Pallas kernels, on_device(): pl.pallas_call(kernel, out_shape=(jax.ShapeDtypeStruct((CH, S), f32), jax...  63.8 us
    unnamed x22, local copies, waits for them, and re-layouts  6.62 us

profile of v1, /device:TPU:1, one launch (start us, length us, event | category | flops | bytes accessed | tf_op | source)
XLA Modules:
  0.0 71.1 jit_solution(11699788183560454557)
XLA Ops:
  0.6 0.0 copy-start.1
  0.6 0.0 copy-start.5
  0.7 0.0 copy-start.7
  0.7 0.0 copy-start.8
  0.7 0.8 %copy.13.embed_ref = f32[64,16]{1,0:T(8,128)S(1)} copy(f32[64,16]{0,1:T(8,128)} %param.17) | data formatting | bytes 8192 | tf_op args[7]
  1.5 0.0 copy-done.1
  1.5 0.0 copy-done.5
  1.5 0.0 copy-done.7
  1.5 0.0 copy-done.8
  1.5 0.0 copy-start
  1.5 1.0 %copy-done = f32[64,2048]{1,0:T(8,128)S(1)} copy-done((f32[64,2048]{1,0:T(8,128)S(1)}, f32[64,2048]{1,0:T(8,128)}, u32[]{:S(2)}) %copy-start) | copy-done | bytes 524312
  2.5 0.0 copy-start.2
  2.6 0.8 %copy-done.2 = f32[64,64]{1,0:T(8,128)S(1)} copy-done((f32[64,64]{1,0:T(8,128)S(1)}, f32[64,64]{1,0:T(8,128)}, u32[]{:S(2)}) %copy-start.2) | copy-done | bytes 16408
  3.3 0.0 copy-start.3
  3.3 0.8 %copy-done.3 = f32[64,64]{1,0:T(8,128)S(1)} copy-done((f32[64,64]{1,0:T(8,128)S(1)}, f32[64,64]{1,0:T(8,128)}, u32[]{:S(2)}) %copy-start.3) | copy-done | bytes 16408
  4.1 0.0 copy-start.4
  4.1 0.8 %copy-done.4 = f32[64,128]{1,0:T(8,128)S(1)} copy-done((f32[64,128]{1,0:T(8,128)S(1)}, f32[64,128]{1,0:T(8,128)}, u32[]{:S(2)}) %copy-start.4) | copy-done | bytes 32792
  4.8 0.0 copy-start.6
  4.8 0.7 copy-done.6
  5.5 63.8 %ewald.1 = (f32[64,128]{1,0:T(8,128)S(1)}, f32[3,128]{1,0:T(4,128)S(1)}, f32[64,128]{1,0:T(8,128)S(1)}) custom-call(f32[3,2048]{1,0:T(4,128)S(1)} %copy-done.1, f32[64,2048]{1,0:T(8,128)S(1)} %copy-done, s32[1,2048]{1,0:T(1,128)S(1)} %bitcast.2, s32[8]{0:T(128)S(1)} %copy-done.7, s32[3,256]{1,0:T(4,128)S(1)} %copy-done.6, f32[1,64]{1,0:T(1,128)S(1)} %bitcast.3, ...), custom_call_target="tpu_custom_call" | custom-call | tf_op jit(solution)/shard_map/ewald/pallas_call | solution.py:363
  69.3 0.6 copy.17
  69.9 0.6 copy.18
  70.5 0.6 copy.19
Async XLA Ops:
  0.6 0.8 %copy-start.1 = (f32[3,2048]{1,0:T(4,128)S(1)}, f32[3,2048]{1,0:T(4,128)}, u32[]{:S(2)}) copy-start(f32[3,2048]{1,0:T(4,128)} %pos_ref.1) | copy-start | bytes 73732
  0.6 0.8 %copy-start.5 = (s32[2048]{0:T(1024)S(1)}, s32[2048]{0:T(1024)}, u32[]{:S(2)}) copy-start(s32[2048]{0:T(1024)} %param.12) | copy-start | bytes 24580
  0.7 0.8 %copy-start.7 = (s32[8]{0:T(128)S(1)}, s32[8]{0:T(128)}, u32[]{:S(2)}) copy-start(s32[8]{0:T(128)} %pad_ref.1) | copy-start | bytes 100
  0.7 0.8 %copy-start.8 = (f32[64]{0:T(128)S(1)}, f32[64]{0:T(128)}, u32[]{:S(2)}) copy-start(f32[64]{0:T(128)} %param.15) | copy-start | bytes 772
  1.5 1.0 %copy-start = (f32[64,2048]{1,0:T(8,128)S(1)}, f32[64,2048]{1,0:T(8,128)}, u32[]{:S(2)}) copy-start(f32[64,2048]{1,0:T(8,128)} %feats_ref.1) | copy-start | bytes 1572868
  2.5 0.8 %copy-start.2 = (f32[64,64]{1,0:T(8,128)S(1)}, f32[64,64]{1,0:T(8,128)}, u32[]{:S(2)}) copy-start(f32[64,64]{1,0:T(8,128)} %wq_ref.1) | copy-start | bytes 49156
  3.3 0.8 %copy-start.3 = (f32[64,64]{1,0:T(8,128)S(1)}, f32[64,64]{1,0:T(8,128)}, u32[]{:S(2)}) copy-start(f32[64,64]{1,0:T(8,128)} %wo_ref.1) | copy-start | bytes 49156
  4.1 0.8 %copy-start.4 = (f32[64,128]{1,0:T(8,128)S(1)}, f32[64,128]{1,0:T(8,128)}, u32[]{:S(2)}) copy-start(f32[64,128]{1,0:T(8,128)} %grad_ref.1) | copy-start | bytes 98308
  4.8 0.7 copy-start.6

commit v2 on v1

--- a/solution.py
+++ b/solution.py
@@ -57,17 +57,23 @@
     return lax.dot_general(a, b, (dims, ((), ())), precision=precision, preferred_element_type=f32)
 
 
-def middle_out(i, n):
-    return n // 2 + ((i + 1) // 2) * (1 - 2 * (i % 2))
+def far_first(n):
+    return sorted(range(1, n), key=lambda d: -min(d, n - d))
+
+
+plane_steps = sorted(
+    [(dx, dz) for dx in range(4) for dz in range(8) if dx or dz],
+    key=lambda d: -(min(d[0], 4 - d[0]) + min(d[1], 8 - d[1])),
+)
 
 
 def kernel(
-    pos_ref, feats_ref, species_ref, pad_ref, k_ref, width_ref, wq_ref, embed_ref, wo_ref, grad_ref,
+    pos_hbm, feats_hbm, species_hbm, pad_hbm, k_hbm, width_hbm, wq_hbm, embed_hbm, wo_hbm, grad_hbm,
     message_ref, force_ref, gfeat_ref,
-    feats, kall, kcol, kmat, xmat, mask, t_hi, t_lo, cos_f, sin_f, charge, cots, adjoint,
+    pos_ref, feats, species_ref, pad_ref, k_ref, width_ref, wq_ref, embed_ref, wo_ref, grad_ref,
+    kall, kcol, kmat, xmat, mask, t_hi, t_lo, cos_f, sin_f, charge, cots, adjoint,
     part, core_in, core_sum, ring_in, owned, table, out_y, in_y, out_f, in_f,
-    feats_sem, k_sem, cot_send, cot_recv, core_sem, plane_send, plane_recv, table_send, table_recv,
-    y_send, y_recv, f_send, f_recv,
+    load_sem, k_sem, cot_sem, core_sem, plane_sem, table_sem, y_sem, f_sem,
 ):
     atoms_at = lax.axis_index("atoms")
     kvec_at = lax.axis_index("kvec")
@@ -76,57 +82,54 @@
     x = x_hi * 2 + x_lo
     me = x * 8 + z
 
-    def on_y(other):
-        return (atoms_at, x_lo * 8 + other)
-
-    def on_plane(px, pz):
-        return ((px // 2) * 16 + pz * 2 + core, (px % 2) * 8 + y)
-
+    ys = [(y + d) % 8 for d in far_first(8)]
+    y_peers = [(other, (atoms_at, x_lo * 8 + other)) for other in ys]
+    plane_peers = []
+    for dx, dz in plane_steps:
+        px, pz = (x + dx) % 4, (z + dz) % 8
+        plane_peers.append((px * 8 + pz, ((px // 2) * 16 + pz * 2 + core, (px % 2) * 8 + y)))
     sibling = (atoms_at + 1 - 2 * core, kvec_at)
     partner = (atoms_at, (1 - x_lo) * 8 + y)
 
-    def plane_loop(body):
-        def step(i, _):
-            px = (x + middle_out(i // 8, 4)) % 4
-            pz = (z + middle_out(i % 8, 8)) % 8
-            body(px, pz, px * 8 + pz)
-            return 0
-
-        lax.fori_loop(0, 31, step, 0)
-
-    def y_loop(body):
-        def step(i, _):
-            body((y + middle_out(i, 8)) % 8)
-            return 0
-
-        lax.fori_loop(0, 7, step, 0)
+    barrier = pltpu.get_barrier_semaphore()
+    for device in [d for _, d in y_peers] + [d for _, d in plane_peers] + [sibling]:
+        pl.semaphore_signal(barrier, inc=1, device_id=device, device_id_type=MESH)
+
+    half_atoms = pl.ds(pl.multiple_of(x_lo * A, A), A)
+    loads = {}
+    for n, (name, src, dst) in enumerate([
+        ("k", k_hbm, k_ref),
+        ("pos", pos_hbm, pos_ref),
+        ("pad", pad_hbm, pad_ref),
+        ("feats", feats_hbm.at[:, half_atoms], feats),
+        ("species", species_hbm, species_ref),
+        ("wq", wq_hbm, wq_ref),
+        ("embed", embed_hbm, embed_ref),
+        ("grad", grad_hbm, grad_ref),
+        ("wo", wo_hbm, wo_ref),
+        ("width", width_hbm, width_ref),
+    ]):
+        loads[name] = pltpu.make_async_copy(src, dst, load_sem.at[n])
+        loads[name].start()
 
     def remote(src, dst, send, recv, device):
         return pltpu.make_async_remote_copy(
             src_ref=src, dst_ref=dst, send_sem=send, recv_sem=recv, device_id=device, device_id_type=MESH
         )
 
-    barrier = pltpu.get_barrier_semaphore()
-
-    def greet(device):
-        pl.semaphore_signal(barrier, inc=1, device_id=device, device_id_type=MESH)
-
-    plane_loop(lambda px, pz, p: greet(on_plane(px, pz)))
-    y_loop(lambda other: greet(on_y(other)))
-    greet(sibling)
-
-    feats_copy = pltpu.make_async_copy(
-        feats_ref.at[:, pl.ds(pl.multiple_of(x_lo * A, A), A)], feats, feats_sem
-    )
-    feats_copy.start()
-
+    def wait_bytes(ref, sem):
+        pltpu.make_async_copy(ref, ref, sem).wait()
+
+    loads["k"].wait()
     kall[x_lo] = jnp.concatenate([k_ref[...].astype(f32), jnp.zeros((5, H), f32)], axis=0)
-    pos = pos_ref[:, pl.ds(pl.multiple_of(x_lo * A, A), A)]
+    loads["pos"].wait()
+    pos = pos_ref[:, half_atoms]
     pos = jnp.concatenate([pos, jnp.zeros((5, A), f32)], axis=0)
     pos_hi = pos.astype(bf16).astype(f32)
     pos_mid = (pos - pos_hi).astype(bf16).astype(f32)
     pos_low = (pos - pos_hi) - pos_mid
     xmat[...] = jnp.concatenate([pos_hi, pos_mid, pos_low, jnp.zeros((8, A), f32)], axis=0).astype(bf16)
+    loads["pad"].wait()
     lanes = lax.broadcasted_iota(jnp.int32, (1, 256), 1)
     for block in range(4):
         mask[:, block * 256 : (block + 1) * 256] = (lanes < pad_ref[x_lo * 4 + block]).astype(f32)
@@ -170,112 +173,103 @@
 
     trig_half(x_lo)
 
-    feats_copy.wait()
-    one_hot = (
-        lax.broadcasted_iota(jnp.int32, (16, A), 0) == species_ref[:, pl.ds(pl.multiple_of(x_lo * A, A), A)]
-    ).astype(f32)
+    for name in ("feats", "species", "wq", "embed"):
+        loads[name].wait()
+    one_hot = (lax.broadcasted_iota(jnp.int32, (16, A), 0) == species_ref[:, half_atoms]).astype(f32)
     q_high, q_low = split(
         mask[...]
         * (
             dot(wq_ref[...], feats[...], ((0,), (0,)), exact)
-            + dot(embed_ref[...], one_hot, precision=exact)
+            + dot(embed_ref[...], one_hot, ((0,), (0,)), exact)
         )
     )
     charge[0:CH, :] = q_high
     charge[CH:128, :] = q_low
     factors(0, x_lo, charge)
 
+    for name in ("grad", "wo", "width"):
+        loads[name].wait()
     pl.semaphore_wait(barrier, 39)
 
     k_copy = remote(kall.at[x_lo], kall.at[x_lo], k_sem.at[0], k_sem.at[1], partner)
     k_copy.start()
-
-    def cot_copy(other, slot):
-        return remote(grad_ref, cots.at[slot], cot_send.at[other], cot_recv.at[slot], on_y(other))
-
-    y_loop(lambda other: cot_copy(other, y).start())
+    for _, device in y_peers:
+        remote(grad_ref, cots.at[y], cot_sem.at[0], cot_sem.at[1], device).start()
     cots[y] = grad_ref[...]
 
     remote(kall.at[1 - x_lo], kall.at[1 - x_lo], k_sem.at[0], k_sem.at[1], partner).wait_recv()
     trig_half(1 - x_lo)
     factors(0, 1 - x_lo, charge)
 
-    def core_copy(which, stage, src, dst):
-        return remote(src, dst, core_sem.at[0, which, stage], core_sem.at[1, which, stage], sibling)
-
     own_rows = pl.ds(pl.multiple_of(core * H, H), H)
     other_rows = pl.ds(pl.multiple_of((1 - core) * H, H), H)
 
     def pair_sum_copy(which):
-        return core_copy(which, 0, part.at[which, other_rows, :], core_in.at[which])
+        return remote(
+            part.at[which, other_rows, :], core_in.at[which],
+            core_sem.at[0, which, 0], core_sem.at[1, which, 0], sibling,
+        )
 
     def share_rows(p):
         return pl.ds(pl.multiple_of(p * 8, 8), 8)
-
-    def plane_copy(which, px, pz, p, slot):
-        return remote(
-            core_sum.at[which, share_rows(p), :], ring_in.at[which, slot],
-            plane_send.at[which, p], plane_recv.at[which, slot], on_plane(px, pz),
-        )
 
     def scatter_start(which):
         pair_sum_copy(which).wait_recv()
         core_sum[which] = part[which, own_rows, :] + core_in[which]
-        plane_loop(lambda px, pz, p: plane_copy(which, px, pz, p, me).start())
+        for p, device in plane_peers:
+            remote(
+                core_sum.at[which, share_rows(p), :], ring_in.at[which, me],
+                plane_sem.at[0, which], plane_sem.at[1, which], device,
+            ).start()
         ring_in[which, me] = core_sum[which, share_rows(me), :]
 
-    def table_rows(p):
-        return pl.ds(pl.multiple_of(core * H + p * 8, 8), 8)
-
-    def table_copy(which, px, pz, p, slot):
-        return remote(
-            owned.at[which], table.at[which, table_rows(slot), :],
-            table_send.at[which, p], table_recv.at[which, slot], on_plane(px, pz),
-        )
+    my_rows = pl.ds(pl.multiple_of(core * H + me * 8, 8), 8)
 
     def gather_start(which):
-        plane_loop(lambda px, pz, p: plane_copy(which, px, pz, p, p).wait_recv())
+        wait_bytes(ring_in.at[which, pl.ds(0, 31)], plane_sem.at[1, which])
         total = ring_in[which, 0]
         for p in range(1, 32):
             total = total + ring_in[which, p]
-        wave = two_pi * kcol[table_rows(me), :]
+        wave = two_pi * kcol[my_rows, :]
         square = jnp.sum(wave * wave, axis=1, keepdims=True)
         width = width_ref[...]
         width = jnp.concatenate([width, width], axis=1)
         gain = jnp.exp(-square * width) * 40.0 / (square + 40.0) / 256.0
         owned[which] = gain * total
-        plane_loop(lambda px, pz, p: table_copy(which, px, pz, p, me).start())
-        table[which, table_rows(me), :] = owned[which]
+        for _, device in plane_peers:
+            remote(
+                owned.at[which], table.at[which, my_rows, :],
+                table_sem.at[0, which], table_sem.at[1, which], device,
+            ).start()
+        table[which, my_rows, :] = owned[which]
 
     def pair_share_copy(which, rows):
-        return core_copy(which, 1, table.at[which, rows, :], table.at[which, rows, :])
+        return remote(
+            table.at[which, rows, :], table.at[which, rows, :],
+            core_sem.at[0, which, 1], core_sem.at[1, which, 1], sibling,
+        )
 
     def gather_end(which):
-        plane_loop(lambda px, pz, p: table_copy(which, px, pz, p, p).wait_recv())
+        wait_bytes(table.at[which, pl.ds(0, 31 * 8), :], table_sem.at[1, which])
         pair_share_copy(which, own_rows).start()
         pair_share_copy(which, other_rows).wait_recv()
 
     pair_sum_copy(0).start()
     scatter_start(0)
 
-    y_loop(lambda other: cot_copy(other, other).wait_recv())
+    wait_bytes(cots.at[pl.ds(0, 7)], cot_sem.at[1])
     for s in range(8):
         cols = slice(s * S, (s + 1) * S)
         high, low = split(mask[:, cols] * dot(wo_ref[...], cots[s], precision=exact))
         adjoint[0:CH, cols] = high
         adjoint[CH:128, cols] = low
-    factors(1, 0, adjoint)
-    factors(1, 1, adjoint)
+    factors(1, 1 - core, adjoint)
     pair_sum_copy(1).start()
+    factors(1, core, adjoint)
     scatter_start(1)
 
     gather_start(0)
     gather_start(1)
-
-    def y_copy(which, other, slot):
-        return remote(
-            out_y.at[which, other], in_y.at[which, slot], y_send.at[which, other], y_recv.at[which, slot], on_y(other)
-        )
 
     def fields(which):
         high, low = split(table[which].T)
@@ -292,7 +286,10 @@
             field = both[0:CH] + both[CH:128]
             out_y[which, 2 * at] = field[:, 0:S]
             out_y[which, 2 * at + 1] = field[:, S:256]
-        y_loop(lambda other: y_copy(which, other, y).start())
+        for other, device in y_peers:
+            remote(
+                out_y.at[which, other], in_y.at[which, y], y_sem.at[0, which], y_sem.at[1, which], device
+            ).start()
         in_y[which, y] = out_y[which, y]
 
     def forces(which, quant, add):
@@ -315,44 +312,42 @@
                 here = rows[:, half * S : (half + 1) * S]
                 out_f[slot] = out_f[slot] + here if add else here
 
-    def f_copy(other, slot):
-        return remote(out_f.at[other], in_f.at[slot], f_send.at[other], f_recv.at[slot], on_y(other))
-
     gather_end(0)
     fields(0)
     forces(0, adjoint, False)
     gather_end(1)
     fields(1)
     forces(1, charge, True)
-    y_loop(lambda other: f_copy(other, y).start())
+    for other, device in y_peers:
+        remote(out_f.at[other], in_f.at[y], f_sem.at[0], f_sem.at[1], device).start()
     in_f[y] = out_f[y]
 
     share = mask[:, pl.ds(pl.multiple_of(y * S, S), S)]
 
     def collect(which):
-        y_loop(lambda other: y_copy(which, other, other).wait_recv())
+        wait_bytes(in_y.at[which, pl.ds(0, 7)], y_sem.at[1, which])
         total = in_y[which, 0]
         for s in range(1, 8):
             total = total + in_y[which, s]
         return share * total
 
     message_ref[...] = dot(wo_ref[...], collect(0), ((0,), (0,)), exact)
-    gfeat_ref[...] = dot(wq_ref[...], collect(1), precision=exact)
-    y_loop(lambda other: f_copy(other, other).wait_recv())
+    wait_bytes(in_f.at[pl.ds(0, 7)], f_sem.at[1])
     total = in_f[0]
     for s in range(1, 8):
         total = total + in_f[s]
     force_ref[...] = (two_pi * total)[0:3, :]
+    gfeat_ref[...] = dot(wq_ref[...], collect(1), precision=exact)
 
     k_copy.wait_send()
-    y_loop(lambda other: cot_copy(other, y).wait_send())
+    wait_bytes(cots.at[pl.ds(0, 7)], cot_sem.at[0])
     for which in range(2):
         pair_sum_copy(which).wait_send()
         pair_share_copy(which, own_rows).wait_send()
-        plane_loop(lambda px, pz, p: plane_copy(which, px, pz, p, me).wait_send())
-        plane_loop(lambda px, pz, p: table_copy(which, px, pz, p, me).wait_send())
-        y_loop(lambda other: y_copy(which, other, y).wait_send())
-    y_loop(lambda other: f_copy(other, y).wait_send())
+        wait_bytes(ring_in.at[which, pl.ds(0, 31)], plane_sem.at[0, which])
+        wait_bytes(table.at[which, pl.ds(0, 31 * 8), :], table_sem.at[0, which])
+        wait_bytes(in_y.at[which, pl.ds(0, 7)], y_sem.at[0, which])
+    wait_bytes(in_f.at[pl.ds(0, 7)], f_sem.at[0])
 
 
 def on_device(
@@ -367,16 +362,19 @@
             jax.ShapeDtypeStruct((3, S), f32),
             jax.ShapeDtypeStruct((CH, S), f32),
         ),
-        in_specs=[
-            vmem,
-            pl.BlockSpec(memory_space=pl.ANY),
-            vmem,
-            pl.BlockSpec(memory_space=pltpu.SMEM),
-            vmem, vmem, vmem, vmem, vmem, vmem,
-        ],
+        in_specs=[pl.BlockSpec(memory_space=pl.ANY)] * 10,
         out_specs=(vmem, vmem, vmem),
         scratch_shapes=[
+            pltpu.VMEM((3, 2 * A), f32),
             pltpu.VMEM((CH, A), f32),
+            pltpu.VMEM((1, 2 * A), jnp.int32),
+            pltpu.SMEM((8,), jnp.int32),
+            pltpu.VMEM((3, H), jnp.int32),
+            pltpu.VMEM((1, CH), f32),
+            pltpu.VMEM((CH, CH), f32),
+            pltpu.VMEM((16, CH), f32),
+            pltpu.VMEM((CH, CH), f32),
+            pltpu.VMEM((CH, S), f32),
             pltpu.VMEM((2, 8, H), f32),
             pltpu.VMEM((K, 8), f32),
             pltpu.VMEM((K, 32), bf16),
@@ -399,17 +397,16 @@
             pltpu.VMEM((2, 8, CH, S), f32),
             pltpu.VMEM((8, 8, S), f32),
             pltpu.VMEM((8, 8, S), f32),
-            dma, dma((2,)), dma((8,)), dma((8,)), dma((2, 2, 2)),
-            dma((2, 32)), dma((2, 32)), dma((2, 32)), dma((2, 32)),
-            dma((2, 8)), dma((2, 8)), dma((8,)), dma((8,)),
+            dma((10,)), dma((2,)), dma((2,)), dma((2, 2, 2)),
+            dma((2, 2)), dma((2, 2)), dma((2, 2)), dma((2,)),
         ],
         name="ewald",
         compiler_params=pltpu.CompilerParams(
-            collective_id=0, has_side_effects=True, vmem_limit_bytes=40 * 1024 * 1024
+            collective_id=0, has_side_effects=True, vmem_limit_bytes=60 * 1024 * 1024
         ),
     )(
         positions, feats, species.reshape(1, -1), pad_count, k_lattice, filter_width.reshape(1, -1),
-        w_charge, species_embed, w_out, grad_out,
+        w_charge, species_embed.T, w_out, grad_out,
     )
 
 

time: 71.6 us -> 58.4 us (0.82)
  Pallas kernels: 63.8 us -> 54.9 us
  local copies, waits for them, and re-layouts: 6.62 us -> 2.58 us
    pallas_call x1, Pallas kernels: 63.8 us -> 54.9 us  [on_device(): pl.pallas_call(kernel, out_shape=(jax.ShapeDtypeStruct((CH, S), f32), jax...]
    unnamed x22 -> x7, local copies, waits for them, and re-layouts: 6.62 us -> 2.58 us
where the time goes in v2:
time: 58.4 us; the launch traced here: 58.2 us
  Pallas kernels  54.9 us (94%)
  local copies, waits for them, and re-layouts  2.58 us (4%)
  between operations  0.66 us (1%)
    pallas_call x1, Pallas kernels, on_device(): pl.pallas_call(kernel, out_shape=(jax.ShapeDtypeStruct((CH, S), f32), jax...  54.9 us
    unnamed x7, local copies, waits for them, and re-layouts  2.58 us

profile of v2, /device:TPU:1, one launch (start us, length us, event | category | flops | bytes accessed | tf_op | source)
XLA Modules:
  0.0 58.2 jit_solution(17464058630983830177)
XLA Ops:
  0.6 54.9 %ewald.1 = (f32[64,128]{1,0:T(8,128)}, f32[3,128]{1,0:T(4,128)}, f32[64,128]{1,0:T(8,128)}) custom-call(f32[3,2048]{1,0:T(4,128)} %pos_hbm.1, f32[64,2048]{1,0:T(8,128)} %feats_hbm.1, s32[1,2048]{1,0:T(1,128)} %bitcast.3, s32[8]{0:T(128)} %pad_hbm.1, s32[3,256]{1,0:T(4,128)} %k_hbm.1, f32[1,64]{1,0:T(1,128)} %bitcast.5, f32[64,64]{1,0:T(8,128)} %wq_hbm.1, ...), custom_call_target="tpu_custom_call" | custom-call | tf_op jit(solution)/shard_map/ewald/pallas_call | solution.py:358
  55.6 0.0 copy-start.1
  55.6 0.0 copy-start
  55.6 1.4 %copy.16 = f32[64,128]{1,0:T(8,128)} copy(f32[64,128]{1,0:T(8,128)} %get-tuple-element.6) | data formatting | bytes 65536
  57.0 0.0 copy-done.1
  57.0 0.6 copy.17
  57.5 0.0 copy-done
  57.5 0.6 %copy.18 = f32[64,128]{1,0:T(8,128)} copy(f32[64,128]{1,0:T(8,128)S(1)} %copy-done) | data formatting | bytes 65536
Async XLA Ops:
  55.6 1.4 %copy-start.1 = (f32[3,128]{1,0:T(4,128)S(1)}, f32[3,128]{1,0:T(4,128)}, u32[]{:S(2)}) copy-start(f32[3,128]{1,0:T(4,128)} %get-tuple-element.7) | copy-start | bytes 4612
  55.6 2.0 %copy-start = (f32[64,128]{1,0:T(8,128)S(1)}, f32[64,128]{1,0:T(8,128)}, u32[]{:S(2)}) copy-start(f32[64,128]{1,0:T(8,128)} %get-tuple-element.8) | copy-start | bytes 98308

commit v3 on v2

v3 whole, which is shorter than its diff:
```python
import functools
import math

import jax
import jax.numpy as jnp
import numpy as np
from jax import lax
from jax.experimental import pallas as pl
from jax.experimental.pallas import tpu as pltpu
from jax.sharding import PartitionSpec as P

MESH = pl.DeviceIdType.MESH
exact = lax.Precision.HIGHEST
two_pi = 2.0 * math.pi
f32 = jnp.float32
bf16 = jnp.bfloat16

A = 1024
K = 512
H = 256
CH = 64
S = 128


def fit_poly(fn, count, points=2000):
    nodes = 0.25 * (np.cos(np.pi * (np.arange(points) + 0.5) / points) + 1.0) * 0.5
    table = np.vander(nodes / 0.25, count, increasing=True)
    coef = np.linalg.lstsq(table, fn(np.sqrt(nodes)), rcond=None)[0]
    return [float(c) / 0.25**n for n, c in enumerate(coef)]


sin_coef = fit_poly(lambda u: 2.0 * np.sin(np.pi * u) / u, 5)
cos_coef = fit_poly(lambda u: np.cos(np.pi * u), 5)


def horner(coef, sq):
    total = coef[-1]
    for c in coef[-2::-1]:
        total = total * sq + c
    return total


def sin_cos_turns(t):
    u = t - jnp.round(t)
    sq = u * u
    twice_sin = u * horner(sin_coef, sq)
    cos_half = horner(cos_coef, sq)
    return 1.0 - 0.5 * (twice_sin * twice_sin), twice_sin * cos_half


def split(value):
    high = value.astype(bf16)
    return high, (value - high.astype(f32)).astype(bf16)


def dot(a, b, dims=((1,), (0,)), precision=None):
    return lax.dot_general(a, b, (dims, ((), ())), precision=precision, preferred_element_type=f32)


def ring(d, n):
    return min(d, n - d)


y_steps = sorted(range(1, 8), key=lambda d: -ring(d, 8))
plane_steps = sorted(
    [(dx, dz) for dx in range(4) for dz in range(8) if dx or dz],
    key=lambda d: -(ring(d[0], 4) + ring(d[1], 8)),
)
y_order = (0, 1, 7, 2, 6, 3, 5, 4)


def kernel(
    pos_hbm, feats_hbm, species_hbm, pad_hbm, k_hbm, width_hbm, wq_hbm, embed_hbm, wo_hbm, grad_hbm,
    message_ref, force_ref, gfeat_ref,
    pos_ref, feats, species_ref, pad_ref, k_ref, width_ref, wq_ref, embed_ref, wo_ref,
    kall, kcol, kmat, xmat, mask, t_hi, t_lo, e_hi, e_lo, cos_f, sin_f, charge, far_charge, cots, adjoint,
    part_h, part_e, in_h, in_e, sum_h, sum_e, ring_h, ring_e, owned, table, out_y, in_y, out_f, in_f,
    load_sem, k_sem, cot_sem, core_sem, plane_sem, table_sem, share_sem, y_sem, f_sem,
    y_ready, plane_ready, k_ready, core_ready,
):
    atoms_at = lax.axis_index("atoms")
    kvec_at = lax.axis_index("kvec")
    core, z, x_hi = atoms_at % 2, (atoms_at // 2) % 8, atoms_at // 16
    x_lo, y = kvec_at // 8, kvec_at % 8
    x = x_hi * 2 + x_lo
    me = z * 4 + x

    def on_y(other):
        return (atoms_at, x_lo * 8 + other)

    def on_plane(px, pz):
        return ((px // 2) * 16 + pz * 2 + core, (px % 2) * 8 + y)

    def on_place(place):
        return on_plane(place % 4, place // 4)

    y_peers = [((y + d) % 8, on_y((y + d) % 8)) for d in y_steps]
    plane_peers = []
    group_peers = []
    for dx, dz in plane_steps:
        px, pz = (x + dx) % 4, (z + dz) % 8
        plane_peers.append((pz * 4 + px, on_plane(px, pz)))
        if dx % 2 == 0:
            group_peers.append(((px // 2) * 8 + pz, on_plane(px, pz)))
    group_me = x_hi * 8 + z
    sibling = (atoms_at + 1 - 2 * core, kvec_at)
    partner = (atoms_at, (1 - x_lo) * 8 + y)

    def remote(src, dst, send, recv, device):
        return pltpu.make_async_remote_copy(
            src_ref=src, dst_ref=dst, send_sem=send, recv_sem=recv, device_id=device, device_id_type=MESH
        )

    def signal(sem, device):
        pl.semaphore_signal(sem, inc=1, device_id=device, device_id_type=MESH)

    def wait_bytes(ref, sem):
        pltpu.make_async_copy(ref, ref, sem).wait()

    barrier = pltpu.get_barrier_semaphore()
    late = y // 5
    y_rank = (1 - late) * (2 * y - 1) + late * (16 - 2 * y)
    y_before = y_rank + (8 - y) // 8
    for i, other in enumerate(y_order):
        if i:

            @pl.when(i > y_rank)
            def _(other=other):
                signal(barrier, on_y(other))

    lax.fori_loop(me + 1, 32, lambda p, _: (signal(barrier, on_place(p)), 0)[1], 0)

    @pl.when(core == 1)
    def _():
        signal(barrier, sibling)

    loads = {}
    for n, (name, src, dst) in enumerate([
        ("k", k_hbm, k_ref),
        ("pos", pos_hbm, pos_ref),
        ("pad", pad_hbm, pad_ref),
        ("feats", feats_hbm, feats),
        ("species", species_hbm, species_ref),
        ("wq", wq_hbm, wq_ref),
        ("embed", embed_hbm, embed_ref),
        ("wo", wo_hbm, wo_ref),
        ("width", width_hbm, width_ref),
        ("grad", grad_hbm, cots.at[y]),
    ]):
        loads[name] = pltpu.make_async_copy(src, dst, load_sem.at[n])
        loads[name].start()

    before = y_before + me + 1 - core

    @pl.when(before > 0)
    def _():
        pl.semaphore_wait(barrier, before)

    for i, other in enumerate(y_order[:-1]):

        @pl.when(i < y_rank)
        def _(other=other):
            signal(y_ready.at[y], on_y(other))

    @pl.when(x_lo == 1)
    def _():
        signal(k_ready, partner)

    def cot_copy(device):
        return remote(grad_hbm, cots.at[y], cot_sem.at[0], cot_sem.at[1], device)

    for i, other in enumerate(y_order[:-1]):

        @pl.when(i < y_rank)
        def _(other=other):
            cot_copy(on_y(other)).start()

    @pl.when(core == 0)
    def _():
        signal(core_ready, sibling)

    loads["k"].wait()
    kall[x_lo] = jnp.concatenate([k_ref[...].astype(f32), jnp.zeros((5, H), f32)], axis=0)
    k_copy = remote(kall.at[x_lo], kall.at[x_lo], k_sem.at[0], k_sem.at[1], partner)

    @pl.when(x_lo == 1)
    def _():
        k_copy.start()

    lax.fori_loop(0, me, lambda p, _: (signal(plane_ready, on_place(p)), 0)[1], 0)

    halves = [pl.ds(pl.multiple_of(h * A, A), A) for h in (x_lo, 1 - x_lo)]
    loads["pos"].wait()
    loads["pad"].wait()
    lanes = lax.broadcasted_iota(jnp.int32, (1, 256), 1)
    for n, h in enumerate((x_lo, 1 - x_lo)):
        pos = jnp.concatenate([pos_ref[:, halves[n]], jnp.zeros((5, A), f32)], axis=0)
        pos_hi = pos.astype(bf16).astype(f32)
        pos_mid = (pos - pos_hi).astype(bf16).astype(f32)
        pos_low = (pos - pos_hi) - pos_mid
        xmat[n] = jnp.concatenate([pos_hi, pos_mid, pos_low, jnp.zeros((8, A), f32)], axis=0).astype(bf16)
        for block in range(4):
            mask[n, :, block * 256 : (block + 1) * 256] = (lanes < pad_ref[h * 4 + block]).astype(f32)

    def set_k(q):
        kt = kall[q].T
        kcol[pl.ds(pl.multiple_of(q * H, H), H), :] = kt
        kmat[pl.ds(pl.multiple_of(q * H, H), H), :] = jnp.concatenate([kt] * 4, axis=1).astype(bf16)

    def trig(q, n, high_ref, low_ref, cos_base, sin_base, keep):
        def step(i, _):
            rows = pl.ds(pl.multiple_of(q * H + i * 32, 32), 32)
            cos_rows = pl.ds(pl.multiple_of(cos_base + i * 32, 32), 32)
            sin_rows = pl.ds(pl.multiple_of(sin_base + i * 32, 32), 32)
            left = kmat[rows, :]
            for at in range(4):
                cols = slice(at * 256, (at + 1) * 256)
                cos, sin = sin_cos_turns(dot(left, xmat[n, :, cols]))
                if keep:
                    cos_f[rows, cols] = cos
                    sin_f[rows, cols] = sin
                high_ref[cos_rows, cols], low_ref[cos_rows, cols] = split(cos)
                high_ref[sin_rows, cols], low_ref[sin_rows, cols] = split(sin)
            return 0

        lax.fori_loop(0, H // 32, step, 0)

    low_lanes = lax.broadcasted_iota(jnp.int32, (1, 128), 1) < CH

    def factors(out_ref, base, terms):
        for i in range(2):
            found = []
            for sine in (0, 1):
                one = jnp.zeros((128, 128), f32)
                for high_ref, low_ref, cos_base, sin_base, quant in terms:
                    rows = pl.ds(pl.multiple_of((sin_base if sine else cos_base) + i * 128, 128), 128)
                    one = one + dot(high_ref[rows, :], quant[...], ((1,), (1,)))
                    one = one + dot(low_ref[rows, :], quant[...], ((1,), (1,)))
                found.append(one + pltpu.roll(one, CH, 1))
            out_ref[pl.ds(pl.multiple_of(base + i * 128, 128), 128), :] = jnp.where(low_lanes, found[0], found[1])

    set_k(x_lo)
    trig(x_lo, 0, t_hi, t_lo, x_lo * H, K + x_lo * H, True)

    for name in ("feats", "species", "wq", "embed"):
        loads[name].wait()
    for n, quant in enumerate((charge, far_charge)):
        one_hot = (lax.broadcasted_iota(jnp.int32, (16, A), 0) == species_ref[:, halves[n]]).astype(f32)
        quant[0:CH, :], quant[CH:128, :] = split(
            mask[n]
            * (
                dot(wq_ref[...], feats[:, halves[n]], ((0,), (0,)), exact)
                + dot(embed_ref[...], one_hot, ((0,), (0,)), exact)
            )
        )

    @pl.when(x_lo == 0)
    def _():
        pl.semaphore_wait(k_ready, 1)
        k_copy.start()

    trig(x_lo, 1, e_hi, e_lo, 0, H, False)
    factors(
        part_h, 0, [(t_hi, t_lo, x_lo * H, K + x_lo * H, charge), (e_hi, e_lo, 0, H, far_charge)]
    )

    h_pair = remote(part_h, in_h, core_sem.at[0], core_sem.at[1], sibling)

    @pl.when(core == 1)
    def _():
        pl.semaphore_wait(core_ready, 1)
        h_pair.start()

    for i, other in enumerate(y_order):
        if i:

            @pl.when(i > y_rank)
            def _(other=other):
                pl.semaphore_wait(y_ready.at[other], 1)
                cot_copy(on_y(other)).start()

    remote(kall.at[1 - x_lo], kall.at[1 - x_lo], k_sem.at[0], k_sem.at[1], partner).wait_recv()
    set_k(1 - x_lo)
    trig(1 - x_lo, 0, t_hi, t_lo, (1 - x_lo) * H, K + (1 - x_lo) * H, True)

    def gain_of(first):
        wave = two_pi * kcol[pl.ds(pl.multiple_of(first, 16), 16), :]
        square = jnp.sum(wave * wave, axis=1, keepdims=True)
        width = width_ref[...]
        width = jnp.concatenate([width, width], axis=1)
        return jnp.exp(-square * width) * 40.0 / (square + 40.0) / 256.0

    def scatter(total, peers, ring_ref, mine):
        for p, device in peers:
            remote(
                total.at[pl.ds(pl.multiple_of(p * 16, 16), 16), :], ring_ref.at[mine],
                plane_sem.at[0], plane_sem.at[1], device,
            ).start()
        ring_ref[mine] = total[pl.ds(pl.multiple_of(mine * 16, 16), 16), :]

    def gather(which, first, ring_ref, count):
        wait_bytes(ring_ref.at[pl.ds(0, count - 1)], plane_sem.at[1])
        total = ring_ref[0]
        for p in range(1, count):
            total = total + ring_ref[p]
        owned[...] = gain_of(first) * total
        rows = pl.ds(pl.multiple_of(first, 16), 16)
        for _, device in plane_peers:
            remote(owned, table.at[which, rows, :], table_sem.at[0], table_sem.at[1], device).start()
        table[which, rows, :] = owned[...]

    def share_copy(which):
        return remote(table.at[which], table.at[which], share_sem.at[0], share_sem.at[1], sibling)

    def share(which):
        wait_bytes(table.at[which, pl.ds(0, 31 * 16), :], table_sem.at[1])
        share_copy(which).start()

    @pl.when(me < 31)
    def _():
        pl.semaphore_wait(plane_ready, 31 - me)

    @pl.when(core == 0)
    def _():
        h_pair.wait_recv()
        sum_h[...] = part_h[...] + in_h[...]
        scatter(sum_h, group_peers, ring_h, group_me)

    for name in ("wo", "width", "grad"):
        loads[name].wait()
    wait_bytes(cots.at[pl.ds(0, 7)], cot_sem.at[1])
    for s in range(8):
        cols = slice(s * S, (s + 1) * S)
        adjoint[0:CH, cols], adjoint[CH:128, cols] = split(
            mask[0, :, cols] * dot(wo_ref[...], cots[s], precision=exact)
        )

    def e_pair(q):
        rows = pl.ds(q * H, H)
        return remote(part_e.at[rows, :], in_e.at[rows, :], core_sem.at[0], core_sem.at[1], sibling)

    for q in range(2):
        factors(part_e, q * H, [(t_hi, t_lo, q * H, K + q * H, adjoint)])

        @pl.when(core == 0)
        def _(q=q):
            e_pair(q).start()

    @pl.when(core == 1)
    def _():
        wait_bytes(in_e, core_sem.at[1])
        sum_e[...] = part_e[...] + in_e[...]
        scatter(sum_e, plane_peers, ring_e, me)

    @pl.when(core == 0)
    def _():
        gather(0, x_lo * H + group_me * 16, ring_h, 16)

    @pl.when(core == 1)
    def _():
        gather(1, me * 16, ring_e, 32)

    def fields(which):
        high, low = split(table[which].T)
        left = jnp.concatenate(
            [
                jnp.concatenate([high[0:CH], high[CH:128]], axis=1),
                jnp.concatenate([low[0:CH], low[CH:128]], axis=1),
            ],
            axis=0,
        )
        for at in range(4):
            cols = slice(at * 256, (at + 1) * 256)
            both = dot(left, t_hi[:, cols]) + dot(left, t_lo[:, cols])
            field = both[0:CH] + both[CH:128]
            out_y[which, 2 * at] = field[:, 0:S]
            out_y[which, 2 * at + 1] = field[:, S:256]
        for other, device in y_peers:
            remote(
                out_y.at[which, other], in_y.at[which, y], y_sem.at[0, which], y_sem.at[1, which], device
            ).start()
        in_y[which, y] = out_y[which, y]

    def forces(which, quant, add):
        high, low = split(table[which])
        high, low = high.astype(f32), low.astype(f32)
        sin_side = jnp.where(low_lanes, pltpu.roll(high, CH, 1), low).astype(bf16)
        cos_side = jnp.where(low_lanes, high, pltpu.roll(low, CH, 1)).astype(bf16)
        sin_side = jnp.concatenate([sin_side, sin_side], axis=1)
        cos_side = jnp.concatenate([cos_side, cos_side], axis=1)
        columns = [kcol[:, n : n + 1] for n in range(3)]
        for at in range(4):
            cols = slice(at * 256, (at + 1) * 256)
            high_q, low_q = quant[0:CH, cols], quant[CH:128, cols]
            right = jnp.concatenate([high_q, high_q, low_q, low_q], axis=0)
            turn = cos_f[:, cols] * dot(sin_side, right) - sin_f[:, cols] * dot(cos_side, right)
            rows = [jnp.sum(column * turn, axis=0, keepdims=True) for column in columns]
            rows = jnp.concatenate(rows + [jnp.zeros((5, 256), f32)], axis=0)
            for half in range(2):
                slot = 2 * at + half
                here = rows[:, half * S : (half + 1) * S]
                out_f[slot] = out_f[slot] + here if add else here

    @pl.when(core == 0)
    def _():
        share(0)

    @pl.when(core == 1)
    def _():
        share_copy(0).wait_recv()

    fields(0)
    forces(0, adjoint, False)

    @pl.when(core == 1)
    def _():
        share(1)

    @pl.when(core == 0)
    def _():
        share_copy(1).wait_recv()

    fields(1)
    forces(1, charge, True)
    for other, device in y_peers:
        remote(out_f.at[other], in_f.at[y], f_sem.at[0], f_sem.at[1], device).start()
    in_f[y] = out_f[y]

    mine = mask[0, :, pl.ds(pl.multiple_of(y * S, S), S)]

    def collect(which):
        wait_bytes(in_y.at[which, pl.ds(0, 7)], y_sem.at[1, which])
        total = in_y[which, 0]
        for s in range(1, 8):
            total = total + in_y[which, s]
        return mine * total

    message_ref[...] = dot(wo_ref[...], collect(0), ((0,), (0,)), exact)
    wait_bytes(in_f.at[pl.ds(0, 7)], f_sem.at[1])
    total = in_f[0]
    for s in range(1, 8):
        total = total + in_f[s]
    force_ref[...] = (two_pi * total)[0:3, :]
    gfeat_ref[...] = dot(wq_ref[...], collect(1), precision=exact)

    k_copy.wait_send()
    wait_bytes(cots.at[pl.ds(0, 7)], cot_sem.at[0])

    @pl.when(core == 0)
    def _():
        wait_bytes(in_e, core_sem.at[0])
        wait_bytes(ring_h.at[pl.ds(0, 15)], plane_sem.at[0])
        share_copy(0).wait_send()

    @pl.when(core == 1)
    def _():
        h_pair.wait_send()
        wait_bytes(ring_e.at[pl.ds(0, 31)], plane_sem.at[0])
        share_copy(1).wait_send()

    wait_bytes(table.at[0, pl.ds(0, 31 * 16), :], table_sem.at[0])
    for which in range(2):
        wait_bytes(in_y.at[which, pl.ds(0, 7)], y_sem.at[0, which])
    wait_bytes(in_f.at[pl.ds(0, 7)], f_sem.at[0])


def on_device(
    positions, feats, species, pad_count, k_lattice, filter_width, w_charge, species_embed, w_out, grad_out
):
    vmem = pl.BlockSpec(memory_space=pltpu.VMEM)
    dma = pltpu.SemaphoreType.DMA
    regular = pltpu.SemaphoreType.REGULAR
    return pl.pallas_call(
        kernel,
        out_shape=(
            jax.ShapeDtypeStruct((CH, S), f32),
            jax.ShapeDtypeStruct((3, S), f32),
            jax.ShapeDtypeStruct((CH, S), f32),
        ),
        in_specs=[pl.BlockSpec(memory_space=pl.ANY)] * 10,
        out_specs=(vmem, vmem, vmem),
        scratch_shapes=[
            pltpu.VMEM((3, 2 * A), f32),
            pltpu.VMEM((CH, 2 * A), f32),
            pltpu.VMEM((1, 2 * A), jnp.int32),
            pltpu.SMEM((8,), jnp.int32),
            pltpu.VMEM((3, H), jnp.int32),
            pltpu.VMEM((1, CH), f32),
            pltpu.VMEM((CH, CH), f32),
            pltpu.VMEM((16, CH), f32),
            pltpu.VMEM((CH, CH), f32),
            pltpu.VMEM((2, 8, H), f32),
            pltpu.VMEM((K, 8), f32),
            pltpu.VMEM((K, 32), bf16),
            pltpu.VMEM((2, 32, A), bf16),
            pltpu.VMEM((2, 1, A), f32),
            pltpu.VMEM((2 * K, A), bf16),
            pltpu.VMEM((2 * K, A), bf16),
            pltpu.VMEM((2 * H, A), bf16),
            pltpu.VMEM((2 * H, A), bf16),
            pltpu.VMEM((K, A), f32),
            pltpu.VMEM((K, A), f32),
            pltpu.VMEM((128, A), bf16),
            pltpu.VMEM((128, A), bf16),
            pltpu.VMEM((8, CH, S), f32),
            pltpu.VMEM((128, A), bf16),
            pltpu.VMEM((H, 128), f32),
            pltpu.VMEM((K, 128), f32),
            pltpu.VMEM((H, 128), f32),
            pltpu.VMEM((K, 128), f32),
            pltpu.VMEM((H, 128), f32),
            pltpu.VMEM((K, 128), f32),
            pltpu.VMEM((16, 16, 128), f32),
            pltpu.VMEM((32, 16, 128), f32),
            pltpu.VMEM((16, 128), f32),
            pltpu.VMEM((2, K, 128), f32),
            pltpu.VMEM((2, 8, CH, S), f32),
            pltpu.VMEM((2, 8, CH, S), f32),
            pltpu.VMEM((8, 8, S), f32),
            pltpu.VMEM((8, 8, S), f32),
            dma((10,)), dma((2,)), dma((2,)), dma((2,)),
            dma((2,)), dma((2,)), dma((2,)), dma((2, 2)), dma((2,)),
            regular((8,)), regular, regular, regular,
        ],
        name="ewald",
        compiler_params=pltpu.CompilerParams(
            collective_id=0, has_side_effects=True, vmem_limit_bytes=60 * 1024 * 1024
        ),
    )(
        positions, feats, species.reshape(1, -1), pad_count, k_lattice, filter_width.reshape(1, -1),
        w_charge, species_embed.T, w_out, grad_out,
    )


def solution(mesh):
    placed = (
        P(None, "atoms"),
        P(None, "atoms"),
        P("atoms"),
        P("atoms"),
        P(None, "kvec"),
        P(),
        P(),
        P(),
        P(),
        P(None, ("atoms", "kvec")),
    )
    return jax.shard_map(
        on_device,
        mesh=mesh,
        in_specs=placed,
        out_specs=(P(None, ("atoms", "kvec")),) * 3,
        check_vma=False,
    )
```

time: 58.4 us -> 61.4 us (1.051)
  Pallas kernels: 54.9 us -> 58 us
    pallas_call x1, Pallas kernels: 54.9 us -> 58 us  [on_device(): pl.pallas_call(kernel, out_shape=(jax.ShapeDtypeStruct((CH, S), f32), jax...]
where the time goes in v3:
time: 61.4 us; the launch traced here: 61.2 us
  Pallas kernels  58 us (94%)
  local copies, waits for them, and re-layouts  2.58 us (4%)
  between operations  0.66 us (1%)
    pallas_call x1, Pallas kernels, on_device(): pl.pallas_call(kernel, out_shape=(jax.ShapeDtypeStruct((CH, S), f32), jax...  58 us
    unnamed x7, local copies, waits for them, and re-layouts  2.58 us

profile of v3, /device:TPU:1, one launch (start us, length us, event | category | flops | bytes accessed | tf_op | source)
XLA Modules:
  0.0 61.2 jit_solution(16009298697183626108)
XLA Ops:
  0.6 58.0 %ewald.1 = (f32[64,128]{1,0:T(8,128)}, f32[3,128]{1,0:T(4,128)}, f32[64,128]{1,0:T(8,128)}) custom-call(f32[3,2048]{1,0:T(4,128)} %pos_hbm.1, f32[64,2048]{1,0:T(8,128)} %feats_hbm.1, s32[1,2048]{1,0:T(1,128)} %bitcast.3, s32[8]{0:T(128)} %pad_hbm.1, s32[3,256]{1,0:T(4,128)} %k_hbm.1, f32[1,64]{1,0:T(1,128)} %bitcast.5, f32[64,64]{1,0:T(8,128)} %wq_hbm.1, ...), custom_call_target="tpu_custom_call" | custom-call | tf_op jit(solution)/shard_map/ewald/pallas_call | solution.py:473
  58.6 0.0 copy-start.1
  58.6 0.0 copy-start
  58.6 1.4 %copy.16 = f32[64,128]{1,0:T(8,128)} copy(f32[64,128]{1,0:T(8,128)} %get-tuple-element.6) | data formatting | bytes 65536
  60.0 0.0 copy-done.1
  60.0 0.6 copy.17
  60.6 0.0 copy-done
  60.6 0.6 %copy.18 = f32[64,128]{1,0:T(8,128)} copy(f32[64,128]{1,0:T(8,128)S(1)} %copy-done) | data formatting | bytes 65536
Async XLA Ops:
  58.6 1.4 %copy-start.1 = (f32[3,128]{1,0:T(4,128)S(1)}, f32[3,128]{1,0:T(4,128)}, u32[]{:S(2)}) copy-start(f32[3,128]{1,0:T(4,128)} %get-tuple-element.7) | copy-start | bytes 4612
  58.6 2.0 %copy-start = (f32[64,128]{1,0:T(8,128)S(1)}, f32[64,128]{1,0:T(8,128)}, u32[]{:S(2)}) copy-start(f32[64,128]{1,0:T(8,128)} %get-tuple-element.8) | copy-start | bytes 98308

commit v4 on v3

--- a/solution.py
+++ b/solution.py
@@ -66,6 +66,7 @@
     [(dx, dz) for dx in range(4) for dz in range(8) if dx or dz],
     key=lambda d: -(ring(d[0], 4) + ring(d[1], 8)),
 )
+plane_far = [int(ring(dz, 8) > 2) for _, dz in plane_steps]
 y_order = (0, 1, 7, 2, 6, 3, 5, 4)
 
 
@@ -84,6 +85,9 @@
     x_lo, y = kvec_at // 8, kvec_at % 8
     x = x_hi * 2 + x_lo
     me = z * 4 + x
+    group_me = x_hi * 8 + z
+    x_at = x_lo * 2 + x_hi
+    place = x_at * 8 + z
 
     def on_y(other):
         return (atoms_at, x_lo * 8 + other)
@@ -91,18 +95,17 @@
     def on_plane(px, pz):
         return ((px // 2) * 16 + pz * 2 + core, (px % 2) * 8 + y)
 
-    def on_place(place):
-        return on_plane(place % 4, place // 4)
+    def on_start(p):
+        return on_plane(p % 4, p // 4)
 
     y_peers = [((y + d) % 8, on_y((y + d) % 8)) for d in y_steps]
     plane_peers = []
     group_peers = []
     for dx, dz in plane_steps:
         px, pz = (x + dx) % 4, (z + dz) % 8
-        plane_peers.append((pz * 4 + px, on_plane(px, pz)))
+        plane_peers.append((((px % 2) * 2 + px // 2) * 8 + pz, on_plane(px, pz)))
         if dx % 2 == 0:
             group_peers.append(((px // 2) * 8 + pz, on_plane(px, pz)))
-    group_me = x_hi * 8 + z
     sibling = (atoms_at + 1 - 2 * core, kvec_at)
     partner = (atoms_at, (1 - x_lo) * 8 + y)
 
@@ -128,7 +131,7 @@
             def _(other=other):
                 signal(barrier, on_y(other))
 
-    lax.fori_loop(me + 1, 32, lambda p, _: (signal(barrier, on_place(p)), 0)[1], 0)
+    lax.fori_loop(me + 1, 32, lambda p, _: (signal(barrier, on_start(p)), 0)[1], 0)
 
     @pl.when(core == 1)
     def _():
@@ -187,7 +190,7 @@
     def _():
         k_copy.start()
 
-    lax.fori_loop(0, me, lambda p, _: (signal(plane_ready, on_place(p)), 0)[1], 0)
+    lax.fori_loop(0, me, lambda p, _: (signal(plane_ready, on_start(p)), 0)[1], 0)
 
     halves = [pl.ds(pl.multiple_of(h * A, A), A) for h in (x_lo, 1 - x_lo)]
     loads["pos"].wait()
@@ -242,6 +245,19 @@
     set_k(x_lo)
     trig(x_lo, 0, t_hi, t_lo, x_lo * H, K + x_lo * H, True)
 
+    @pl.when(x_lo == 0)
+    def _():
+        pl.semaphore_wait(k_ready, 1)
+        k_copy.start()
+
+    for i, other in enumerate(y_order):
+        if i:
+
+            @pl.when(i > y_rank)
+            def _(other=other):
+                pl.semaphore_wait(y_ready.at[other], 1)
+                cot_copy(on_y(other)).start()
+
     for name in ("feats", "species", "wq", "embed"):
         loads[name].wait()
     for n, quant in enumerate((charge, far_charge)):
@@ -254,11 +270,6 @@
             )
         )
 
-    @pl.when(x_lo == 0)
-    def _():
-        pl.semaphore_wait(k_ready, 1)
-        k_copy.start()
-
     trig(x_lo, 1, e_hi, e_lo, 0, H, False)
     factors(
         part_h, 0, [(t_hi, t_lo, x_lo * H, K + x_lo * H, charge), (e_hi, e_lo, 0, H, far_charge)]
@@ -270,14 +281,6 @@
     def _():
         pl.semaphore_wait(core_ready, 1)
         h_pair.start()
-
-    for i, other in enumerate(y_order):
-        if i:
-
-            @pl.when(i > y_rank)
-            def _(other=other):
-                pl.semaphore_wait(y_ready.at[other], 1)
-                cot_copy(on_y(other)).start()
 
     remote(kall.at[1 - x_lo], kall.at[1 - x_lo], k_sem.at[0], k_sem.at[1], partner).wait_recv()
     set_k(1 - x_lo)
@@ -298,23 +301,22 @@
             ).start()
         ring_ref[mine] = total[pl.ds(pl.multiple_of(mine * 16, 16), 16), :]
 
-    def gather(which, first, ring_ref, count):
+    def gather(which, ring_ref, count):
         wait_bytes(ring_ref.at[pl.ds(0, count - 1)], plane_sem.at[1])
         total = ring_ref[0]
         for p in range(1, count):
             total = total + ring_ref[p]
-        owned[...] = gain_of(first) * total
-        rows = pl.ds(pl.multiple_of(first, 16), 16)
-        for _, device in plane_peers:
-            remote(owned, table.at[which, rows, :], table_sem.at[0], table_sem.at[1], device).start()
-        table[which, rows, :] = owned[...]
-
-    def share_copy(which):
-        return remote(table.at[which], table.at[which], share_sem.at[0], share_sem.at[1], sibling)
+        owned[...] = gain_of(place * 16) * total
+        for (_, device), far in zip(plane_peers, plane_far):
+            remote(owned, table.at[which, x_at, z], table_sem.at[0], table_sem.at[1 + far], device).start()
+        table[which, x_at, z] = owned[...]
 
     def share(which):
-        wait_bytes(table.at[which, pl.ds(0, 31 * 16), :], table_sem.at[1])
-        share_copy(which).start()
+        for far, steps in enumerate(((0, 1, 7, 2, 6), (3, 5, 4))):
+            wait_bytes(ring_e.at[pl.ds(0, 4 * len(steps) - (1 - far))], table_sem.at[1 + far])
+            for step in steps:
+                rows = table.at[which, :, (z + step) % 8]
+                remote(rows, rows, share_sem.at[0], share_sem.at[1], sibling).start()
 
     @pl.when(me < 31)
     def _():
@@ -350,18 +352,23 @@
     def _():
         wait_bytes(in_e, core_sem.at[1])
         sum_e[...] = part_e[...] + in_e[...]
-        scatter(sum_e, plane_peers, ring_e, me)
+        scatter(sum_e, plane_peers, ring_e, place)
 
     @pl.when(core == 0)
     def _():
-        gather(0, x_lo * H + group_me * 16, ring_h, 16)
-
-    @pl.when(core == 1)
-    def _():
-        gather(1, me * 16, ring_e, 32)
+        gather(0, ring_h, 16)
+
+    @pl.when(core == 1)
+    def _():
+        gather(1, ring_e, 32)
+
+    def y_copy(which, other):
+        return remote(
+            out_y.at[which, other], in_y.at[which, y], y_sem.at[0, which], y_sem.at[1, which], on_y(other)
+        )
 
     def fields(which):
-        high, low = split(table[which].T)
+        high, low = split(table[which].reshape(K, 128).T)
         left = jnp.concatenate(
             [
                 jnp.concatenate([high[0:CH], high[CH:128]], axis=1),
@@ -369,20 +376,26 @@
             ],
             axis=0,
         )
-        for at in range(4):
-            cols = slice(at * 256, (at + 1) * 256)
+        for turn in (2, 1, 3, 0):
+            at = (y // 2 + turn) % 4
+            cols = pl.ds(pl.multiple_of(at * 256, 256), 256)
             both = dot(left, t_hi[:, cols]) + dot(left, t_lo[:, cols])
             field = both[0:CH] + both[CH:128]
-            out_y[which, 2 * at] = field[:, 0:S]
-            out_y[which, 2 * at + 1] = field[:, S:256]
-        for other, device in y_peers:
-            remote(
-                out_y.at[which, other], in_y.at[which, y], y_sem.at[0, which], y_sem.at[1, which], device
-            ).start()
+            for n in range(2):
+                other = 2 * at + n
+                out_y[which, other] = field[:, n * S : (n + 1) * S]
+                if turn:
+                    y_copy(which, other).start()
+                else:
+
+                    @pl.when(other != y)
+                    def _(other=other):
+                        y_copy(which, other).start()
+
         in_y[which, y] = out_y[which, y]
 
     def forces(which, quant, add):
-        high, low = split(table[which])
+        high, low = split(table[which].reshape(K, 128))
         high, low = high.astype(f32), low.astype(f32)
         sin_side = jnp.where(low_lanes, pltpu.roll(high, CH, 1), low).astype(bf16)
         cos_side = jnp.where(low_lanes, high, pltpu.roll(low, CH, 1)).astype(bf16)
@@ -407,7 +420,7 @@
 
     @pl.when(core == 1)
     def _():
-        share_copy(0).wait_recv()
+        wait_bytes(table.at[0], share_sem.at[1])
 
     fields(0)
     forces(0, adjoint, False)
@@ -418,7 +431,7 @@
 
     @pl.when(core == 0)
     def _():
-        share_copy(1).wait_recv()
+        wait_bytes(table.at[1], share_sem.at[1])
 
     fields(1)
     forces(1, charge, True)
@@ -450,15 +463,15 @@
     def _():
         wait_bytes(in_e, core_sem.at[0])
         wait_bytes(ring_h.at[pl.ds(0, 15)], plane_sem.at[0])
-        share_copy(0).wait_send()
+        wait_bytes(table.at[0], share_sem.at[0])
 
     @pl.when(core == 1)
     def _():
         h_pair.wait_send()
         wait_bytes(ring_e.at[pl.ds(0, 31)], plane_sem.at[0])
-        share_copy(1).wait_send()
-
-    wait_bytes(table.at[0, pl.ds(0, 31 * 16), :], table_sem.at[0])
+        wait_bytes(table.at[1], share_sem.at[0])
+
+    wait_bytes(ring_e.at[pl.ds(0, 31)], table_sem.at[0])
     for which in range(2):
         wait_bytes(in_y.at[which, pl.ds(0, 7)], y_sem.at[0, which])
     wait_bytes(in_f.at[pl.ds(0, 7)], f_sem.at[0])
@@ -470,13 +483,17 @@
     vmem = pl.BlockSpec(memory_space=pltpu.VMEM)
     dma = pltpu.SemaphoreType.DMA
     regular = pltpu.SemaphoreType.REGULAR
-    return pl.pallas_call(
+    operands = [
+        pltpu.with_memory_space_constraint(array, pltpu.HBM)
+        for array in (
+            positions, feats, species.reshape(1, -1), pad_count, k_lattice, filter_width.reshape(1, -1),
+            w_charge, species_embed.T, w_out, grad_out,
+        )
+    ]
+    shapes = ((CH, S), (3, S), (CH, S))
+    results = pl.pallas_call(
         kernel,
-        out_shape=(
-            jax.ShapeDtypeStruct((CH, S), f32),
-            jax.ShapeDtypeStruct((3, S), f32),
-            jax.ShapeDtypeStruct((CH, S), f32),
-        ),
+        out_shape=tuple(pltpu.VMEM(shape, f32) for shape in shapes),
         in_specs=[pl.BlockSpec(memory_space=pl.ANY)] * 10,
         out_specs=(vmem, vmem, vmem),
         scratch_shapes=[
@@ -513,23 +530,39 @@
             pltpu.VMEM((16, 16, 128), f32),
             pltpu.VMEM((32, 16, 128), f32),
             pltpu.VMEM((16, 128), f32),
-            pltpu.VMEM((2, K, 128), f32),
+            pltpu.VMEM((2, 4, 8, 16, 128), f32),
             pltpu.VMEM((2, 8, CH, S), f32),
             pltpu.VMEM((2, 8, CH, S), f32),
             pltpu.VMEM((8, 8, S), f32),
             pltpu.VMEM((8, 8, S), f32),
             dma((10,)), dma((2,)), dma((2,)), dma((2,)),
-            dma((2,)), dma((2,)), dma((2,)), dma((2, 2)), dma((2,)),
+            dma((2,)), dma((3,)), dma((2,)), dma((2, 2)), dma((2,)),
             regular((8,)), regular, regular, regular,
         ],
         name="ewald",
         compiler_params=pltpu.CompilerParams(
-            collective_id=0, has_side_effects=True, vmem_limit_bytes=60 * 1024 * 1024
+            collective_id=0, has_side_effects=True, vmem_limit_bytes=32 * 1024 * 1024
         ),
-    )(
-        positions, feats, species.reshape(1, -1), pad_count, k_lattice, filter_width.reshape(1, -1),
-        w_charge, species_embed.T, w_out, grad_out,
-    )
+    )(*operands)
+    return pl.pallas_call(
+        put_away,
+        out_shape=tuple(jax.ShapeDtypeStruct(shape, f32) for shape in shapes),
+        in_specs=[vmem] * 3,
+        out_specs=(pl.BlockSpec(memory_space=pl.ANY),) * 3,
+        scratch_shapes=[dma((3,))],
+        name="put_away",
+    )(*results)
+
+
+def put_away(message, force, gfeat, message_out, force_out, gfeat_out, sem):
+    copies = [
+        pltpu.make_async_copy(src, dst, sem.at[n])
+        for n, (src, dst) in enumerate(((message, message_out), (force, force_out), (gfeat, gfeat_out)))
+    ]
+    for copy in copies:
+        copy.start()
+    for copy in copies:
+        copy.wait()
 
 
 def solution(mesh):

time: 61.4 us -> 58.6 us (0.954)
  Pallas kernels: 58 us -> 56 us
  local copies, waits for them, and re-layouts: 2.58 us -> 1.78 us
    pallas_call x1 -> x2, Pallas kernels: 58 us -> 56 us  [the longest x1 54.6 us: on_device(): pl.pallas_call(kernel, out_shape=tuple((pltpu.VMEM(shape, f32) for shape...]
    unnamed x7 -> x6, local copies, waits for them, and re-layouts: 2.58 us -> 1.78 us
where the time goes in v4:
time: 58.6 us; the launch traced here: 58.4 us
  Pallas kernels  56 us (96%)
  local copies, waits for them, and re-layouts  1.78 us (3%)
  between operations  0.65 us (1%)
    pallas_call x1, Pallas kernels, on_device(): pl.pallas_call(kernel, out_shape=tuple((pltpu.VMEM(shape, f32) for shape...  54.6 us
    unnamed x6, local copies, waits for them, and re-layouts  1.78 us
    pallas_call x1, Pallas kernels, on_device(): pl.pallas_call(put_away, out_shape=tuple((jax.ShapeDtypeStruct(shape, f32...  1.43 us

profile of v4, /device:TPU:1, one launch (start us, length us, event | category | flops | bytes accessed | tf_op | source)
XLA Modules:
  0.0 58.4 jit_solution(5975429141586750371)
XLA Ops:
  0.6 54.6 %ewald.1 = (f32[64,128]{1,0:T(8,128)S(1)}, f32[3,128]{1,0:T(4,128)S(1)}, f32[64,128]{1,0:T(8,128)S(1)}) custom-call(f32[3,2048]{1,0:T(4,128)} %pos_hbm.1, f32[64,2048]{1,0:T(8,128)} %feats_hbm.1, s32[1,2048]{1,0:T(1,128)} %bitcast.3, s32[8]{0:T(128)} %pad_hbm.1, s32[3,256]{1,0:T(4,128)} %k_hbm.1, f32[1,64]{1,0:T(1,128)} %bitcast.5, f32[64,64]{1,0:T(8,128)} %wq_hbm.1, ...), custom_call_target="tpu_custom_call" | custom-call | tf_op jit(solution)/shard_map/ewald/pallas_call | solution.py:494
  55.2 0.0 copy-start
  55.2 0.6 %copy-done = f32[64,128]{1,0:T(8,128)} copy-done((f32[64,128]{1,0:T(8,128)}, f32[64,128]{1,0:T(8,128)S(1)}, u32[]{:S(2)}) %copy-start) | copy-done | bytes 32792
  55.8 0.0 copy-start.1
  55.8 0.6 %copy-done.1 = f32[64,128]{1,0:T(8,128)} copy-done((f32[64,128]{1,0:T(8,128)}, f32[64,128]{1,0:T(8,128)S(1)}, u32[]{:S(2)}) %copy-start.1) | copy-done | bytes 32792
  56.4 0.0 copy-start.2
  56.4 0.6 copy-done.2
  57.0 1.4 %put_away.1 = (f32[64,128]{1,0:T(8,128)}, f32[3,128]{1,0:T(4,128)}, f32[64,128]{1,0:T(8,128)}) custom-call(f32[64,128]{1,0:T(8,128)} %copy-done, f32[3,128]{1,0:T(4,128)} %copy-done.2, f32[64,128]{1,0:T(8,128)} %copy-done.1), custom_call_target="tpu_custom_call" | custom-call | tf_op jit(solution)/shard_map/put_away/pallas_call | solution.py:547
Async XLA Ops:
  55.2 0.6 %copy-start = (f32[64,128]{1,0:T(8,128)}, f32[64,128]{1,0:T(8,128)S(1)}, u32[]{:S(2)}) copy-start(f32[64,128]{1,0:T(8,128)S(1)} %get-tuple-element.6.message) | copy-start | bytes 98308
  55.8 0.6 %copy-start.1 = (f32[64,128]{1,0:T(8,128)}, f32[64,128]{1,0:T(8,128)S(1)}, u32[]{:S(2)}) copy-start(f32[64,128]{1,0:T(8,128)S(1)} %get-tuple-element.8.gfeat) | copy-start | bytes 98308
  56.4 0.6 %copy-start.2 = (f32[3,128]{1,0:T(4,128)}, f32[3,128]{1,0:T(4,128)S(1)}, u32[]{:S(2)}) copy-start(f32[3,128]{1,0:T(4,128)S(1)} %get-tuple-element.7.force) | copy-start | bytes 4612

commit v5 on v4

--- a/solution.py
+++ b/solution.py
@@ -76,7 +76,7 @@
     pos_ref, feats, species_ref, pad_ref, k_ref, width_ref, wq_ref, embed_ref, wo_ref,
     kall, kcol, kmat, xmat, mask, t_hi, t_lo, e_hi, e_lo, cos_f, sin_f, charge, far_charge, cots, adjoint,
     part_h, part_e, in_h, in_e, sum_h, sum_e, ring_h, ring_e, owned, table, out_y, in_y, out_f, in_f,
-    load_sem, k_sem, cot_sem, core_sem, plane_sem, table_sem, share_sem, y_sem, f_sem,
+    load_sem, k_sem, cot_send, cot_recv, core_sem, plane_sem, table_sem, share_sem, y_sem, f_sem,
     y_ready, plane_ready, k_ready, core_ready,
 ):
     atoms_at = lax.axis_index("atoms")
@@ -169,14 +169,17 @@
     def _():
         signal(k_ready, partner)
 
-    def cot_copy(device):
-        return remote(grad_hbm, cots.at[y], cot_sem.at[0], cot_sem.at[1], device)
+    def cot_copy(src, slot, other):
+        return remote(src, cots.at[slot], cot_send, cot_recv.at[slot], on_y(other))
+
+    def near(other):
+        return (other - y + 10) % 8 <= 4
 
     for i, other in enumerate(y_order[:-1]):
 
-        @pl.when(i < y_rank)
+        @pl.when((i < y_rank) & near(other))
         def _(other=other):
-            cot_copy(on_y(other)).start()
+            cot_copy(grad_hbm, y, other).start()
 
     @pl.when(core == 0)
     def _():
@@ -253,10 +256,10 @@
     for i, other in enumerate(y_order):
         if i:
 
-            @pl.when(i > y_rank)
+            @pl.when((i > y_rank) & near(other))
             def _(other=other):
                 pl.semaphore_wait(y_ready.at[other], 1)
-                cot_copy(on_y(other)).start()
+                cot_copy(grad_hbm, y, other).start()
 
     for name in ("feats", "species", "wq", "embed"):
         loads[name].wait()
@@ -270,7 +273,34 @@
             )
         )
 
+    def rank_of(other):
+        late = other // 5
+        return (1 - late) * (2 * other - 1) + late * (16 - 2 * other)
+
+    def cot_wait(slot):
+        wait_bytes(cots.at[slot], cot_recv.at[slot])
+
+    def pass_on(back, targets):
+        slot = (y + back) % 8
+        cot_wait(slot)
+        for step in targets:
+            cot_copy(cots.at[slot], slot, (y + step) % 8).start()
+
+    routes = ((6, (2, 1)), (2, (7,)))
+    for back, targets in routes:
+
+        @pl.when(rank_of((y + back) % 8) < y_rank)
+        def _(back=back, targets=targets):
+            pass_on(back, targets)
+
     trig(x_lo, 1, e_hi, e_lo, 0, H, False)
+
+    for back, targets in routes:
+
+        @pl.when(rank_of((y + back) % 8) > y_rank)
+        def _(back=back, targets=targets):
+            pass_on(back, targets)
+
     factors(
         part_h, 0, [(t_hi, t_lo, x_lo * H, K + x_lo * H, charge), (e_hi, e_lo, 0, H, far_charge)]
     )
@@ -322,15 +352,17 @@
     def _():
         pl.semaphore_wait(plane_ready, 31 - me)
 
-    @pl.when(core == 0)
-    def _():
-        h_pair.wait_recv()
-        sum_h[...] = part_h[...] + in_h[...]
-        scatter(sum_h, group_peers, ring_h, group_me)
+    for i, other in enumerate(y_order):
+        if i:
+
+            @pl.when((i > y_rank) & jnp.logical_not(near(other)))
+            def _(other=other):
+                pl.semaphore_wait(y_ready.at[other], 1)
 
     for name in ("wo", "width", "grad"):
         loads[name].wait()
-    wait_bytes(cots.at[pl.ds(0, 7)], cot_sem.at[1])
+    for step in (1, 7, 3, 5, 4):
+        cot_wait((y + step) % 8)
     for s in range(8):
         cols = slice(s * S, (s + 1) * S)
         adjoint[0:CH, cols], adjoint[CH:128, cols] = split(
@@ -347,6 +379,12 @@
         @pl.when(core == 0)
         def _(q=q):
             e_pair(q).start()
+
+    @pl.when(core == 0)
+    def _():
+        h_pair.wait_recv()
+        sum_h[...] = part_h[...] + in_h[...]
+        scatter(sum_h, group_peers, ring_h, group_me)
 
     @pl.when(core == 1)
     def _():
@@ -457,7 +495,7 @@
     gfeat_ref[...] = dot(wq_ref[...], collect(1), precision=exact)
 
     k_copy.wait_send()
-    wait_bytes(cots.at[pl.ds(0, 7)], cot_sem.at[0])
+    wait_bytes(cots.at[pl.ds(0, 7)], cot_send)
 
     @pl.when(core == 0)
     def _():
@@ -535,7 +573,7 @@
             pltpu.VMEM((2, 8, CH, S), f32),
             pltpu.VMEM((8, 8, S), f32),
             pltpu.VMEM((8, 8, S), f32),
-            dma((10,)), dma((2,)), dma((2,)), dma((2,)),
+            dma((10,)), dma((2,)), dma, dma((8,)), dma((2,)),
             dma((2,)), dma((3,)), dma((2,)), dma((2, 2)), dma((2,)),
             regular((8,)), regular, regular, regular,
         ],
@@ -551,7 +589,8 @@
         out_specs=(pl.BlockSpec(memory_space=pl.ANY),) * 3,
         scratch_shapes=[dma((3,))],
         name="put_away",
-    )(*results)
+        compiler_params=pltpu.CompilerParams(vmem_limit_bytes=1024 * 1024),
+    )(*[pltpu.with_memory_space_constraint(array, pltpu.VMEM) for array in results])
 
 
 def put_away(message, force, gfeat, message_out, force_out, gfeat_out, sem):

time: 58.6 us -> 62.8 us (1.072)
  Pallas kernels: 56 us -> 62.1 us
  local copies, waits for them, and re-layouts: 1.78 us -> 0 us
    pallas_call x1, Pallas kernels: 54.6 us -> 61.4 us  [on_device(): pl.pallas_call(kernel, out_shape=tuple((pltpu.VMEM(shape, f32) for shape...]
    unnamed x6 -> x0, local copies, waits for them, and re-layouts: 1.78 us -> none
    pallas_call x1, Pallas kernels: 1.43 us -> 0.66 us  [on_device(): pl.pallas_call(put_away, out_shape=tuple((jax.ShapeDtypeStruct(shape, f32...]
where the time goes in v5:
time: 62.8 us; the launch traced here: 62.7 us
  Pallas kernels  62.1 us (99%)
  between operations  0.64 us (1%)
    pallas_call x1, Pallas kernels, on_device(): pl.pallas_call(kernel, out_shape=tuple((pltpu.VMEM(shape, f32) for shape...  61.4 us

profile of v5, /device:TPU:1, one launch (start us, length us, event | category | flops | bytes accessed | tf_op | source)
XLA Modules:
  0.0 62.7 jit_solution(2597996340490527825)
XLA Ops:
  0.6 61.4 %ewald.1 = (f32[64,128]{1,0:T(8,128)S(1)}, f32[3,128]{1,0:T(4,128)S(1)}, f32[64,128]{1,0:T(8,128)S(1)}) custom-call(f32[3,2048]{1,0:T(4,128)} %pos_hbm.1, f32[64,2048]{1,0:T(8,128)} %feats_hbm.1, s32[1,2048]{1,0:T(1,128)} %bitcast.3, s32[8]{0:T(128)} %pad_hbm.1, s32[3,256]{1,0:T(4,128)} %k_hbm.1, f32[1,64]{1,0:T(1,128)} %bitcast.5, f32[64,64]{1,0:T(8,128)} %wq_hbm.1, ...), custom_call_target="tpu_custom_call" | custom-call | tf_op jit(solution)/shard_map/ewald/pallas_call | solution.py:532
  62.0 0.7 %put_away.1 = (f32[64,128]{1,0:T(8,128)}, f32[3,128]{1,0:T(4,128)}, f32[64,128]{1,0:T(8,128)}) custom-call(f32[64,128]{1,0:T(8,128)S(1)} %get-tuple-element.6.message, f32[3,128]{1,0:T(4,128)S(1)} %get-tuple-element.7.force, f32[64,128]{1,0:T(8,128)S(1)} %get-tuple-element.8.gfeat), custom_call_target="tpu_custom_call" | custom-call | tf_op jit(solution)/shard_map/put_away/pallas_call | solution.py:585

commit v6 on v4

--- a/solution.py
+++ b/solution.py
@@ -74,9 +74,9 @@
     pos_hbm, feats_hbm, species_hbm, pad_hbm, k_hbm, width_hbm, wq_hbm, embed_hbm, wo_hbm, grad_hbm,
     message_ref, force_ref, gfeat_ref,
     pos_ref, feats, species_ref, pad_ref, k_ref, width_ref, wq_ref, embed_ref, wo_ref,
-    kall, kcol, kmat, xmat, mask, t_hi, t_lo, e_hi, e_lo, cos_f, sin_f, charge, far_charge, cots, adjoint,
+    kall, kcol, kmat, xmat, mask, t_hi, t_lo, e_hi, e_lo, cos_f, sin_f, quants, far_charge, cots, sums_e,
     part_h, part_e, in_h, in_e, sum_h, sum_e, ring_h, ring_e, owned, table, out_y, in_y, out_f, in_f,
-    load_sem, k_sem, cot_sem, core_sem, plane_sem, table_sem, share_sem, y_sem, f_sem,
+    load_sem, k_sem, cot_send, cot_recv, core_sem, plane_sem, table_sem, share_sem, y_sem, f_sem,
     y_ready, plane_ready, k_ready, core_ready,
 ):
     atoms_at = lax.axis_index("atoms")
@@ -170,7 +170,7 @@
         signal(k_ready, partner)
 
     def cot_copy(device):
-        return remote(grad_hbm, cots.at[y], cot_sem.at[0], cot_sem.at[1], device)
+        return remote(grad_hbm, cots.at[y], cot_send, cot_recv.at[y], device)
 
     for i, other in enumerate(y_order[:-1]):
 
@@ -260,7 +260,7 @@
 
     for name in ("feats", "species", "wq", "embed"):
         loads[name].wait()
-    for n, quant in enumerate((charge, far_charge)):
+    for n, quant in enumerate((quants.at[0], far_charge)):
         one_hot = (lax.broadcasted_iota(jnp.int32, (16, A), 0) == species_ref[:, halves[n]]).astype(f32)
         quant[0:CH, :], quant[CH:128, :] = split(
             mask[n]
@@ -272,7 +272,7 @@
 
     trig(x_lo, 1, e_hi, e_lo, 0, H, False)
     factors(
-        part_h, 0, [(t_hi, t_lo, x_lo * H, K + x_lo * H, charge), (e_hi, e_lo, 0, H, far_charge)]
+        part_h, 0, [(t_hi, t_lo, x_lo * H, K + x_lo * H, quants.at[0]), (e_hi, e_lo, 0, H, far_charge)]
     )
 
     h_pair = remote(part_h, in_h, core_sem.at[0], core_sem.at[1], sibling)
@@ -281,10 +281,6 @@
     def _():
         pl.semaphore_wait(core_ready, 1)
         h_pair.start()
-
-    remote(kall.at[1 - x_lo], kall.at[1 - x_lo], k_sem.at[0], k_sem.at[1], partner).wait_recv()
-    set_k(1 - x_lo)
-    trig(1 - x_lo, 0, t_hi, t_lo, (1 - x_lo) * H, K + (1 - x_lo) * H, True)
 
     def gain_of(first):
         wave = two_pi * kcol[pl.ds(pl.multiple_of(first, 16), 16), :]
@@ -328,21 +324,47 @@
         sum_h[...] = part_h[...] + in_h[...]
         scatter(sum_h, group_peers, ring_h, group_me)
 
+    remote(kall.at[1 - x_lo], kall.at[1 - x_lo], k_sem.at[0], k_sem.at[1], partner).wait_recv()
+    set_k(1 - x_lo)
+    trig(1 - x_lo, 0, t_hi, t_lo, (1 - x_lo) * H, K + (1 - x_lo) * H, True)
+
     for name in ("wo", "width", "grad"):
         loads[name].wait()
-    wait_bytes(cots.at[pl.ds(0, 7)], cot_sem.at[1])
-    for s in range(8):
-        cols = slice(s * S, (s + 1) * S)
-        adjoint[0:CH, cols], adjoint[CH:128, cols] = split(
-            mask[0, :, cols] * dot(wo_ref[...], cots[s], precision=exact)
-        )
+
+    def add_pair(turn):
+        pair = (y // 2 + turn) % 4
+        cols = pl.ds(pl.multiple_of(pair * 256, 256), 256)
+        for slot in (2 * pair, 2 * pair + 1):
+            if turn:
+                wait_bytes(cots.at[slot], cot_recv.at[slot])
+            else:
+
+                @pl.when(slot != y)
+                def _(slot=slot):
+                    wait_bytes(cots.at[slot], cot_recv.at[slot])
+
+        block = jnp.concatenate([cots[2 * pair], cots[2 * pair + 1]], axis=1)
+        both = jnp.concatenate(split(mask[0, :, cols] * dot(wo_ref[...], block, precision=exact)), axis=0)
+        quants[1, :, cols] = both
+        for sine in range(2):
+            for i in range(4):
+                rows = slice(sine * K + i * 128, sine * K + (i + 1) * 128)
+                here = slice(i * 128, (i + 1) * 128)
+                one = dot(t_hi[rows, cols], both, ((1,), (1,))) + dot(t_lo[rows, cols], both, ((1,), (1,)))
+                sums_e[sine, here, :] = one + sums_e[sine, here, :] if turn else one
+
+    for turn in (0, 1, 3, 2):
+        add_pair(turn)
 
     def e_pair(q):
         rows = pl.ds(q * H, H)
         return remote(part_e.at[rows, :], in_e.at[rows, :], core_sem.at[0], core_sem.at[1], sibling)
 
     for q in range(2):
-        factors(part_e, q * H, [(t_hi, t_lo, q * H, K + q * H, adjoint)])
+        rows = slice(q * H, (q + 1) * H)
+        found = [sums_e[sine, rows, :] for sine in range(2)]
+        found = [one + pltpu.roll(one, CH, 1) for one in found]
+        part_e[rows, :] = jnp.where(low_lanes, found[0], found[1])
 
         @pl.when(core == 0)
         def _(q=q):
@@ -394,7 +416,7 @@
 
         in_y[which, y] = out_y[which, y]
 
-    def forces(which, quant, add):
+    def forces(which, add):
         high, low = split(table[which].reshape(K, 128))
         high, low = high.astype(f32), low.astype(f32)
         sin_side = jnp.where(low_lanes, pltpu.roll(high, CH, 1), low).astype(bf16)
@@ -404,7 +426,7 @@
         columns = [kcol[:, n : n + 1] for n in range(3)]
         for at in range(4):
             cols = slice(at * 256, (at + 1) * 256)
-            high_q, low_q = quant[0:CH, cols], quant[CH:128, cols]
+            high_q, low_q = quants[1 - which, 0:CH, cols], quants[1 - which, CH:128, cols]
             right = jnp.concatenate([high_q, high_q, low_q, low_q], axis=0)
             turn = cos_f[:, cols] * dot(sin_side, right) - sin_f[:, cols] * dot(cos_side, right)
             rows = [jnp.sum(column * turn, axis=0, keepdims=True) for column in columns]
@@ -414,27 +436,12 @@
                 here = rows[:, half * S : (half + 1) * S]
                 out_f[slot] = out_f[slot] + here if add else here
 
-    @pl.when(core == 0)
-    def _():
-        share(0)
-
-    @pl.when(core == 1)
-    def _():
-        wait_bytes(table.at[0], share_sem.at[1])
-
-    fields(0)
-    forces(0, adjoint, False)
-
-    @pl.when(core == 1)
-    def _():
-        share(1)
-
-    @pl.when(core == 0)
-    def _():
-        wait_bytes(table.at[1], share_sem.at[1])
-
-    fields(1)
-    forces(1, charge, True)
+    share(core)
+    fields(core)
+    forces(core, False)
+    wait_bytes(table.at[1 - core], share_sem.at[1])
+    fields(1 - core)
+    forces(1 - core, True)
     for other, device in y_peers:
         remote(out_f.at[other], in_f.at[y], f_sem.at[0], f_sem.at[1], device).start()
     in_f[y] = out_f[y]
@@ -457,21 +464,20 @@
     gfeat_ref[...] = dot(wq_ref[...], collect(1), precision=exact)
 
     k_copy.wait_send()
-    wait_bytes(cots.at[pl.ds(0, 7)], cot_sem.at[0])
+    wait_bytes(cots.at[pl.ds(0, 7)], cot_send)
 
     @pl.when(core == 0)
     def _():
         wait_bytes(in_e, core_sem.at[0])
         wait_bytes(ring_h.at[pl.ds(0, 15)], plane_sem.at[0])
-        wait_bytes(table.at[0], share_sem.at[0])
 
     @pl.when(core == 1)
     def _():
         h_pair.wait_send()
         wait_bytes(ring_e.at[pl.ds(0, 31)], plane_sem.at[0])
-        wait_bytes(table.at[1], share_sem.at[0])
 
     wait_bytes(ring_e.at[pl.ds(0, 31)], table_sem.at[0])
+    wait_bytes(table.at[core], share_sem.at[0])
     for which in range(2):
         wait_bytes(in_y.at[which, pl.ds(0, 7)], y_sem.at[0, which])
     wait_bytes(in_f.at[pl.ds(0, 7)], f_sem.at[0])
@@ -517,10 +523,10 @@
             pltpu.VMEM((2 * H, A), bf16),
             pltpu.VMEM((K, A), f32),
             pltpu.VMEM((K, A), f32),
-            pltpu.VMEM((128, A), bf16),
+            pltpu.VMEM((2, 128, A), bf16),
             pltpu.VMEM((128, A), bf16),
             pltpu.VMEM((8, CH, S), f32),
-            pltpu.VMEM((128, A), bf16),
+            pltpu.VMEM((2, K, 128), f32),
             pltpu.VMEM((H, 128), f32),
             pltpu.VMEM((K, 128), f32),
             pltpu.VMEM((H, 128), f32),
@@ -535,7 +541,7 @@
             pltpu.VMEM((2, 8, CH, S), f32),
             pltpu.VMEM((8, 8, S), f32),
             pltpu.VMEM((8, 8, S), f32),
-            dma((10,)), dma((2,)), dma((2,)), dma((2,)),
+            dma((10,)), dma((2,)), dma, dma((8,)), dma((2,)),
             dma((2,)), dma((3,)), dma((2,)), dma((2, 2)), dma((2,)),
             regular((8,)), regular, regular, regular,
         ],
@@ -551,7 +557,8 @@
         out_specs=(pl.BlockSpec(memory_space=pl.ANY),) * 3,
         scratch_shapes=[dma((3,))],
         name="put_away",
-    )(*results)
+        compiler_params=pltpu.CompilerParams(vmem_limit_bytes=1024 * 1024),
+    )(*[pltpu.with_memory_space_constraint(array, pltpu.VMEM) for array in results])
 
 
 def put_away(message, force, gfeat, message_out, force_out, gfeat_out, sem):

time: 58.6 us -> 57.2 us (0.976)
  local copies, waits for them, and re-layouts: 1.78 us -> 0 us
    unnamed x6 -> x0, local copies, waits for them, and re-layouts: 1.78 us -> none
    pallas_call x1, Pallas kernels: 54.6 us -> 55.8 us  [on_device(): pl.pallas_call(kernel, out_shape=tuple((pltpu.VMEM(shape, f32) for shape...]
    pallas_call x1, Pallas kernels: 1.43 us -> 0.66 us  [on_device(): pl.pallas_call(put_away, out_shape=tuple((jax.ShapeDtypeStruct(shape, f32...]
where the time goes in v6:
time: 57.2 us; the launch traced here: 57.1 us
  Pallas kernels  56.4 us (99%)
  between operations  0.64 us (1%)
    pallas_call x1, Pallas kernels, on_device(): pl.pallas_call(kernel, out_shape=tuple((pltpu.VMEM(shape, f32) for shape...  55.8 us

profile of v6, /device:TPU:1, one launch (start us, length us, event | category | flops | bytes accessed | tf_op | source)
XLA Modules:
  0.0 57.1 jit_solution(11000404152120992650)
XLA Ops:
  0.6 55.8 %ewald.1 = (f32[64,128]{1,0:T(8,128)S(1)}, f32[3,128]{1,0:T(4,128)S(1)}, f32[64,128]{1,0:T(8,128)S(1)}) custom-call(f32[3,2048]{1,0:T(4,128)} %pos_hbm.1, f32[64,2048]{1,0:T(8,128)} %feats_hbm.1, s32[1,2048]{1,0:T(1,128)} %bitcast.3, s32[8]{0:T(128)} %pad_hbm.1, s32[3,256]{1,0:T(4,128)} %k_hbm.1, f32[1,64]{1,0:T(1,128)} %bitcast.5, f32[64,64]{1,0:T(8,128)} %wq_hbm.1, ...), custom_call_target="tpu_custom_call" | custom-call | tf_op jit(solution)/shard_map/ewald/pallas_call | solution.py:500
  56.4 0.7 %put_away.1 = (f32[64,128]{1,0:T(8,128)}, f32[3,128]{1,0:T(4,128)}, f32[64,128]{1,0:T(8,128)}) custom-call(f32[64,128]{1,0:T(8,128)S(1)} %get-tuple-element.6.message, f32[3,128]{1,0:T(4,128)S(1)} %get-tuple-element.7.force, f32[64,128]{1,0:T(8,128)S(1)} %get-tuple-element.8.gfeat), custom_call_target="tpu_custom_call" | custom-call | tf_op jit(solution)/shard_map/put_away/pallas_call | solution.py:553

commit v7 on v6

--- a/solution.py
+++ b/solution.py
@@ -212,9 +212,9 @@
 
     def trig(q, n, high_ref, low_ref, cos_base, sin_base, keep):
         def step(i, _):
-            rows = pl.ds(pl.multiple_of(q * H + i * 32, 32), 32)
-            cos_rows = pl.ds(pl.multiple_of(cos_base + i * 32, 32), 32)
-            sin_rows = pl.ds(pl.multiple_of(sin_base + i * 32, 32), 32)
+            rows = pl.ds(pl.multiple_of(q * H + i * 128, 128), 128)
+            cos_rows = pl.ds(pl.multiple_of(cos_base + i * 128, 128), 128)
+            sin_rows = pl.ds(pl.multiple_of(sin_base + i * 128, 128), 128)
             left = kmat[rows, :]
             for at in range(4):
                 cols = slice(at * 256, (at + 1) * 256)
@@ -226,7 +226,7 @@
                 high_ref[sin_rows, cols], low_ref[sin_rows, cols] = split(sin)
             return 0
 
-        lax.fori_loop(0, H // 32, step, 0)
+        lax.fori_loop(0, H // 128, step, 0)
 
     low_lanes = lax.broadcasted_iota(jnp.int32, (1, 128), 1) < CH
 
@@ -436,12 +436,27 @@
                 here = rows[:, half * S : (half + 1) * S]
                 out_f[slot] = out_f[slot] + here if add else here
 
-    share(core)
-    fields(core)
-    forces(core, False)
-    wait_bytes(table.at[1 - core], share_sem.at[1])
-    fields(1 - core)
-    forces(1 - core, True)
+    @pl.when(core == 0)
+    def _():
+        share(0)
+
+    @pl.when(core == 1)
+    def _():
+        wait_bytes(table.at[0], share_sem.at[1])
+
+    fields(0)
+    forces(0, False)
+
+    @pl.when(core == 1)
+    def _():
+        share(1)
+
+    @pl.when(core == 0)
+    def _():
+        wait_bytes(table.at[1], share_sem.at[1])
+
+    fields(1)
+    forces(1, True)
     for other, device in y_peers:
         remote(out_f.at[other], in_f.at[y], f_sem.at[0], f_sem.at[1], device).start()
     in_f[y] = out_f[y]

time: 57.2 us -> 54.1 us (0.946)
  Pallas kernels: 56.4 us -> 53.3 us
    pallas_call x1, Pallas kernels: 55.8 us -> 52.7 us  [on_device(): pl.pallas_call(kernel, out_shape=tuple((pltpu.VMEM(shape, f32) for shape...]
where the time goes in v7:
time: 54.1 us; the launch traced here: 54 us
  Pallas kernels  53.3 us (99%)
  between operations  0.64 us (1%)
    pallas_call x1, Pallas kernels, on_device(): pl.pallas_call(kernel, out_shape=tuple((pltpu.VMEM(shape, f32) for shape...  52.7 us

profile of v7, /device:TPU:1, one launch (start us, length us, event | category | flops | bytes accessed | tf_op | source)
XLA Modules:
  0.0 54.0 jit_solution(12362648485572749315)
XLA Ops:
  0.6 52.7 %ewald.1 = (f32[64,128]{1,0:T(8,128)S(1)}, f32[3,128]{1,0:T(4,128)S(1)}, f32[64,128]{1,0:T(8,128)S(1)}) custom-call(f32[3,2048]{1,0:T(4,128)} %pos_hbm.1, f32[64,2048]{1,0:T(8,128)} %feats_hbm.1, s32[1,2048]{1,0:T(1,128)} %bitcast.3, s32[8]{0:T(128)} %pad_hbm.1, s32[3,256]{1,0:T(4,128)} %k_hbm.1, f32[1,64]{1,0:T(1,128)} %bitcast.5, f32[64,64]{1,0:T(8,128)} %wq_hbm.1, ...), custom_call_target="tpu_custom_call" | custom-call | tf_op jit(solution)/shard_map/ewald/pallas_call | solution.py:515
  53.3 0.7 %put_away.1 = (f32[64,128]{1,0:T(8,128)}, f32[3,128]{1,0:T(4,128)}, f32[64,128]{1,0:T(8,128)}) custom-call(f32[64,128]{1,0:T(8,128)S(1)} %get-tuple-element.6.message, f32[3,128]{1,0:T(4,128)S(1)} %get-tuple-element.7.force, f32[64,128]{1,0:T(8,128)S(1)} %get-tuple-element.8.gfeat), custom_call_target="tpu_custom_call" | custom-call | tf_op jit(solution)/shard_map/put_away/pallas_call | solution.py:568

commit v8 on v7

--- a/solution.py
+++ b/solution.py
@@ -66,7 +66,7 @@
     [(dx, dz) for dx in range(4) for dz in range(8) if dx or dz],
     key=lambda d: -(ring(d[0], 4) + ring(d[1], 8)),
 )
-plane_far = [int(ring(dz, 8) > 2) for _, dz in plane_steps]
+plane_far = [int(ring(dz, 8) > 3) for _, dz in plane_steps]
 y_order = (0, 1, 7, 2, 6, 3, 5, 4)
 
 
@@ -75,7 +75,7 @@
     message_ref, force_ref, gfeat_ref,
     pos_ref, feats, species_ref, pad_ref, k_ref, width_ref, wq_ref, embed_ref, wo_ref,
     kall, kcol, kmat, xmat, mask, t_hi, t_lo, e_hi, e_lo, cos_f, sin_f, quants, far_charge, cots, sums_e,
-    part_h, part_e, in_h, in_e, sum_h, sum_e, ring_h, ring_e, owned, table, out_y, in_y, out_f, in_f,
+    part_h, part_e, in_h, in_e, sum_h, sum_e, ring_h, ring_e, gain_ref, owned, table, out_y, in_y, out_f, in_f,
     load_sem, k_sem, cot_send, cot_recv, core_sem, plane_sem, table_sem, share_sem, y_sem, f_sem,
     y_ready, plane_ready, k_ready, core_ready,
 ):
@@ -298,17 +298,18 @@
         ring_ref[mine] = total[pl.ds(pl.multiple_of(mine * 16, 16), 16), :]
 
     def gather(which, ring_ref, count):
+        gain_ref[...] = gain_of(place * 16)
         wait_bytes(ring_ref.at[pl.ds(0, count - 1)], plane_sem.at[1])
         total = ring_ref[0]
         for p in range(1, count):
             total = total + ring_ref[p]
-        owned[...] = gain_of(place * 16) * total
+        owned[...] = gain_ref[...] * total
         for (_, device), far in zip(plane_peers, plane_far):
             remote(owned, table.at[which, x_at, z], table_sem.at[0], table_sem.at[1 + far], device).start()
         table[which, x_at, z] = owned[...]
 
     def share(which):
-        for far, steps in enumerate(((0, 1, 7, 2, 6), (3, 5, 4))):
+        for far, steps in enumerate(((0, 1, 7, 2, 6, 3, 5), (4,))):
             wait_bytes(ring_e.at[pl.ds(0, 4 * len(steps) - (1 - far))], table_sem.at[1 + far])
             for step in steps:
                 rows = table.at[which, :, (z + step) % 8]
@@ -551,6 +552,7 @@
             pltpu.VMEM((16, 16, 128), f32),
             pltpu.VMEM((32, 16, 128), f32),
             pltpu.VMEM((16, 128), f32),
+            pltpu.VMEM((16, 128), f32),
             pltpu.VMEM((2, 4, 8, 16, 128), f32),
             pltpu.VMEM((2, 8, CH, S), f32),
             pltpu.VMEM((2, 8, CH, S), f32),

time: 54.1 us -> 54.1 us (level)
  no operation moved by 1% of the time
where the time goes in v8:
time: 54.1 us; the launch traced here: 53.9 us
  Pallas kernels  53.3 us (99%)
  between operations  0.64 us (1%)
    pallas_call x1, Pallas kernels, on_device(): pl.pallas_call(kernel, out_shape=tuple((pltpu.VMEM(shape, f32) for shape...  52.6 us

profile of v8, /device:TPU:1, one launch (start us, length us, event | category | flops | bytes accessed | tf_op | source)
XLA Modules:
  0.0 53.9 jit_solution(4833922349338944678)
XLA Ops:
  0.6 52.6 %ewald.1 = (f32[64,128]{1,0:T(8,128)S(1)}, f32[3,128]{1,0:T(4,128)S(1)}, f32[64,128]{1,0:T(8,128)S(1)}) custom-call(f32[3,2048]{1,0:T(4,128)} %pos_hbm.1, f32[64,2048]{1,0:T(8,128)} %feats_hbm.1, s32[1,2048]{1,0:T(1,128)} %bitcast.3, s32[8]{0:T(128)} %pad_hbm.1, s32[3,256]{1,0:T(4,128)} %k_hbm.1, f32[1,64]{1,0:T(1,128)} %bitcast.5, f32[64,64]{1,0:T(8,128)} %wq_hbm.1, ...), custom_call_target="tpu_custom_call" | custom-call | tf_op jit(solution)/shard_map/ewald/pallas_call | solution.py:516
  53.3 0.7 %put_away.1 = (f32[64,128]{1,0:T(8,128)}, f32[3,128]{1,0:T(4,128)}, f32[64,128]{1,0:T(8,128)}) custom-call(f32[64,128]{1,0:T(8,128)S(1)} %get-tuple-element.6.message, f32[3,128]{1,0:T(4,128)S(1)} %get-tuple-element.7.force, f32[64,128]{1,0:T(8,128)S(1)} %get-tuple-element.8.gfeat), custom_call_target="tpu_custom_call" | custom-call | tf_op jit(solution)/shard_map/put_away/pallas_call | solution.py:570
